TPU v7x, 512 devices: a whole 4x8x8 slice. The times are simulated.
512 devices in a mesh: replica: 4 (over z_lo, core), dp: 4 (over x), mp: 32 (over y, z_hi).
Axes of the slice: x: 4, y: 8, z: 8 (z_hi: 4, z_lo: 2; z = z_hi * 2 + z_lo), core: 2. Of those that a mesh axis runs over, the one named last changes fastest.
Arguments:
- tokens: bfloat16 [2048, 6144], P(('replica', 'dp'), 'mp'), may hold values from -6 to 6
- norm_gain: bfloat16 [6144], replicated, may hold values from 0.5 to 1.5
- joined_weight: bfloat16 [6144, 21504], P('dp', 'mp'), may hold values from -0.15625 to 0.15625
- output_grad: bfloat16 [2048, 21504], P(('replica', 'dp'), 'mp'), may hold values from -1.5 to 1.5
Outputs:
- activated: bfloat16 [2048, 21504], P(('replica', 'dp'), 'mp')
- normed_grad: bfloat16 [2048, 6144], P(('replica', 'dp'), 'mp')
- weight_grad: bfloat16 [6144, 21504], P('dp', 'mp')
All inputs are finite; a program needn't handle non-finite values.
Results may differ from a plain program's by a relative error of at most 0.02.
Values may be sent and summed in bfloat16 or wider, within the bound.
A program may use at most 64 MiB of HBM per device.

v0:
```python
import jax
import jax.numpy as jnp
from jax import lax
from jax.sharding import PartitionSpec as P

HEADS = 24
HEAD_DIM = 128


contract_rows = (((0,), (0,)), ((), ()))
contract_cols = (((1,), (1,)), ((), ()))


def normalize(inputs, scaling):
    values = inputs.astype(jnp.float32)
    center = jnp.mean(values, axis=1, keepdims=True)
    spread = jnp.mean(jnp.square(values - center), axis=1, keepdims=True)
    return ((values - center) * lax.rsqrt(spread + 1e-06) * scaling.astype(jnp.float32)).astype(
        jnp.bfloat16
    )


def local(tokens, norm_gain, joined_weight, output_grad):
    gathered = lax.all_gather(tokens, "mp", axis=1, tiled=True)
    normed = normalize(gathered, norm_gain)
    own_rows = lax.all_to_all(normed, "dp", split_axis=1, concat_axis=0, tiled=True)
    columns = joined_weight.shape[1]
    full_weight = lax.all_gather(joined_weight, "dp", axis=0, tiled=True)
    projected = jnp.dot(normed, full_weight, preferred_element_type=jnp.float32)
    linear_count = 3 * HEADS * HEAD_DIM // lax.axis_size("mp")
    linear = lax.broadcasted_iota(jnp.int32, (1, columns), 1) < linear_count
    normal_cdf = 0.5 * (1.0 + jax.scipy.special.erf(projected * 0.7071067811865476))
    density = jnp.exp(-0.5 * projected * projected) * 0.3989422804014327
    activated = jnp.where(linear, projected, projected * normal_cdf).astype(jnp.bfloat16)
    slopes = jnp.where(linear, jnp.ones_like(projected), normal_cdf + projected * density)
    inner_grad = (output_grad.astype(jnp.float32) * slopes).astype(jnp.bfloat16)
    every_grad = lax.all_gather(inner_grad, "dp", axis=0, tiled=True)
    local_weight = lax.dot_general(
        own_rows, every_grad, contract_rows, preferred_element_type=jnp.float32
    )
    weight_sum = lax.psum(local_weight.astype(jnp.bfloat16), "replica").astype(jnp.float32)
    weight_grad = (weight_sum / lax.axis_size("replica")).astype(jnp.bfloat16)
    partial_grad = lax.dot_general(
        inner_grad, full_weight, contract_cols, preferred_element_type=jnp.float32
    )
    normed_grad = lax.psum_scatter(
        partial_grad.astype(jnp.bfloat16), "mp", scatter_dimension=1, tiled=True
    )
    return (activated, normed_grad, weight_grad)


def solution(mesh):
    in_specs = (P(("replica", "dp"), "mp"), P(), P("dp", "mp"), P(("replica", "dp"), "mp"))
    out_specs = (P(("replica", "dp"), "mp"), P(("replica", "dp"), "mp"), P("dp", "mp"))
    return jax.shard_map(local, mesh=mesh, in_specs=in_specs, out_specs=out_specs, check_vma=False)
```

profile of v0, /device:TPU:1, one launch (start us, length us, event | category | flops | bytes accessed | tf_op | source)
XLA Modules:
  0.0 520.3 jit_solution(837620178130205067)
XLA Ops:
  7.2 0.0 all-gather.3.cloned.1.call-start
  7.2 0.7 all-gather.3.cloned.1.call-update
  7.9 0.0 all-gather.5.cloned.1.call-start
  7.9 0.7 all-gather.5.cloned.1.call-update
  8.6 0.7 convert_element_type.31
  9.4 89.7 %all-gather.3.cloned.1.call-done = bf16[128,6144]{0,1:T(8,128)(2,1)} async-done(((bf16[128,192]{0,1:T(8,128)(2,1)}), bf16[128,6144]{0,1:T(8,128)(2,1)}) %all-gather.3.cloned.1.call-update) | async-done | bytes 1572880 | tf_op jit(solution)/shard_map/all_gather | solution.py:24
  99.1 0.0 copy-start
  99.1 2.3 convert_reduce_fusion
  101.4 2.2 fusion.2
  103.7 0.0 copy-done
  103.7 1.9 fusion.4
  105.5 0.0 copy-start.1
  105.5 4.1 all-to-all-start
  109.6 0.0 all-reduce.2.cloned.1.call-start
  109.6 22.2 %all-to-all-done = bf16[128,4,1536]{0,2,1:T(8,128)(2,1)S(1)} async-done(((bf16[128,4,1536]{0,2,1:T(8,128)(2,1)}), bf16[128,4,1536]{0,2,1:T(8,128)(2,1)S(1)}, u32[]{:S(2)}, u32[]{:S(2)}) %all-to-all-start) | async-done | bytes 1572896 | tf_op jit(solution)/shard_map/all_to_all | solution.py:26
  131.8 0.7 copy.7
  132.5 64.7 %all-gather.5.cloned.1.call-done = bf16[6144,672]{0,1:T(8,128)(2,1)} async-done(((bf16[1536,672]{0,1:T(8,128)(2,1)}), bf16[6144,672]{0,1:T(8,128)(2,1)}) %all-gather.5.cloned.1.call-update) | async-done | bytes 8257552 | tf_op jit(solution)/shard_map/all_gather | solution.py:28
  197.3 0.0 copy-done.1
  197.3 6.8 %fusion.12 = (bf16[128,672]{0,1:T(8,128)(2,1)S(1)}, bf16[128,672]{0,1:T(8,128)(2,1)}) fusion(bf16[128,672]{0,1:T(8,128)(2,1)S(1)} %copy-done.1, pred[672]{0:T(1024)(128)(4,1)S(1)} %iota_compare_fusion, bf16[6144,672]{0,1:T(8,128)(2,1)} %all-gather.5.cloned.1.call-done, bf16[128,6144]{0,1:T(8,128)(2,1)} %fusion.4), kind=kOutput, calls=%fused_computation.19 | convolution fusion | flops 1058254848 | bytes 10347168 | tf_op jit(solution)/shard_map/dot_general | solution.py:29
  204.0 14.7 %all_gather.11 = bf16[512,672]{0,1:T(8,128)(2,1)S(1)} all-gather(bf16[128,672]{0,1:T(8,128)(2,1)S(1)} %get-tuple-element.3), channel_id=1, replica_groups=mesh['replica'=4,'dp'=4,'mp'=32] {'dp'}, dimensions={0}, use_global_device_ids=true | all-gather | bytes 860160 | tf_op jit(solution)/shard_map/all_gather | solution.py:37
  218.7 2.6 convolution_convert_fusion.1
  221.3 0.0 all-reduce.2.cloned.1.call-update
  221.3 0.0 reduce-scatter.2.cloned.1.call-start
  221.4 8.2 %convolution_convert_fusion = bf16[128,6144]{0,1:T(8,128)(2,1)} fusion(bf16[128,672]{0,1:T(8,128)(2,1)S(1)} %get-tuple-element.3, bf16[6144,672]{0,1:T(8,128)(2,1)} %all-gather.5.cloned.1.call-done), kind=kOutput, calls=%fused_computation | convolution fusion | flops 1057751040 | bytes 10002432 | tf_op jit(solution)/shard_map/dot_general | solution.py:43
  229.6 0.0 reduce-scatter.2.cloned.1.call-update
  229.6 54.3 %all-reduce.2.cloned.1.call-done = bf16[1536,672]{0,1:T(8,128)(2,1)} async-done(((bf16[1536,672]{0,1:T(8,128)(2,1)}), bf16[1536,672]{0,1:T(8,128)(2,1)}) %all-reduce.2.cloned.1.call-update) | async-done | bytes 2064400 | tf_op jit(solution)/shard_map/psum | solution.py:41
  283.9 3.2 multiply_convert_fusion
  287.2 226.6 %reduce-scatter.2.cloned.1.call-done = bf16[128,192]{0,1:T(8,128)(2,1)} async-done(((bf16[128,6144]{0,1:T(8,128)(2,1)}), bf16[128,192]{0,1:T(8,128)(2,1)}) %reduce-scatter.2.cloned.1.call-update) | async-done | bytes 49168 | tf_op jit(solution)/shard_map/reduce_scatter | solution.py:46
  (3 shorter events, 0.0 us)
Async XLA Ops:
  7.2 91.9 %all-gather.3.cloned.1.call-start = ((), (), s32[]{:S(2)}) async-start(), calls=%async_computation.2 | async-start | bytes 1622016 | tf_op jit(solution)/shard_map/all_gather | solution.py:24
  7.9 189.4 %all-gather.5.cloned.1.call-start = ((), (), s32[]{:S(2)}) async-start(), calls=%async_computation.3 | async-start | bytes 10321920 | tf_op jit(solution)/shard_map/all_gather | solution.py:28
  99.1 4.6 copy-start
  105.5 91.7 %copy-start.1 = (bf16[128,672]{0,1:T(8,128)(2,1)S(1)}, bf16[128,672]{0,1:T(8,128)(2,1)}, u32[]{:S(2)}) copy-start(bf16[128,672]{0,1:T(8,128)(2,1)} %param.7) | copy-start | bytes 516100
  105.5 26.3 %all-to-all-start = ((bf16[128,4,1536]{0,2,1:T(8,128)(2,1)}), bf16[128,4,1536]{0,2,1:T(8,128)(2,1)S(1)}, u32[]{:S(2)}, u32[]{:S(2)}) async-start(bf16[128,4,1536]{0,2,1:T(8,128)(2,1)} %bitcast), calls=%async_computation.1 | async-start | bytes 3145728 | tf_op jit(solution)/shard_map/all_to_all | solution.py:26
  109.6 174.3 %all-reduce.2.cloned.1.call-start = ((), (), s32[]{:S(2)}) async-start(), calls=%async_computation.5 | async-start | bytes 4128768 | tf_op jit(solution)/shard_map/psum | solution.py:41
  221.3 292.5 %reduce-scatter.2.cloned.1.call-start = ((), (), s32[]{:S(2)}) async-start(), calls=%async_computation.4 | async-start | bytes 1622016 | tf_op jit(solution)/shard_map/reduce_scatter | solution.py:46
Sparse Core Ops, SparseCore 0:
  11.2 87.8 all-gather.2
  101.2 96.0 all-gather.4
  221.4 62.4 all-reduce.1
  289.5 224.2 reduce-scatter.1
where the time goes:
time: 524 us; the launch traced here: 520 us
  waiting for transfers between devices  459 us (88%)
  matrix products  17.6 us (3%)
  blocking collectives  14.7 us (3%)
  between operations  13.8 us (3%)
  other arithmetic  10.4 us (2%)
    reduce_scatter x1, waiting for transfers between devices, local(): lax.psum_scatter(partial_grad.astype(jnp.bfloat16), 'mp', scatter_dimensi...  227 us
    all_gather x1, waiting for transfers between devices, local(): gathered = lax.all_gather(tokens, 'mp', axis=1, tiled=True)  89.7 us
    all_gather x1, waiting for transfers between devices, local(): full_weight = lax.all_gather(joined_weight, 'dp', axis=0, tiled=True)  64.7 us
    psum x1, waiting for transfers between devices, local(): lax.psum(local_weight.astype(jnp.bfloat16), 'replica').astype(jnp.float32)  54.3 us
    all_to_all x1, waiting for transfers between devices, local(): lax.all_to_all(normed, 'dp', split_axis=1, concat_axis=0, tiled=True)  22.2 us
    all_gather x1, blocking collectives, local(): every_grad = lax.all_gather(inner_grad, 'dp', axis=0, tiled=True)  14.7 us
  transfers between devices with their start and end apart: 5, of which 5 were waited for; matrix products, arithmetic and copies ran while one was open for 4% of the time, Pallas kernels for 0%

commit v1 on v0

v1 whole, which is shorter than its diff:
```python
import functools

import jax
import jax.numpy as jnp
from jax import lax
from jax.experimental import pallas as pl
from jax.experimental.pallas import tpu as pltpu
from jax.sharding import PartitionSpec as P

MESH = pl.DeviceIdType.MESH
F32 = jnp.float32
BF16 = jnp.bfloat16

NX = 4
NY = 8
NZ = 4
TOK = 128
FEAT = 192
HALF = NZ * FEAT
COLS = 672
QKV = 288
D = 6144
CHUNK = 256
SUB = TOK // 2

SEGMENTS = tuple((z * 128, z * FEAT, 128) for z in range(NZ)) + tuple(
    (512 + z * 64, z * FEAT + 128, 64) for z in range(NZ)
)


def remote(src, dst, send_sem, recv_sem, **device):
    return pltpu.make_async_remote_copy(
        src_ref=src,
        dst_ref=dst,
        send_sem=send_sem,
        recv_sem=recv_sem,
        device_id=device,
        device_id_type=MESH,
    )


def lanes_below_64(rows):
    return lax.broadcasted_iota(jnp.int32, (rows, 128), 1) < 64


def merge_stats(stack, features):
    count = stack.shape[0]
    means = stack[:, 0:1, :]
    mean = jnp.sum(means, axis=0) / count
    squares = jnp.sum(stack[:, 1:2, :], axis=0) + features * jnp.sum(
        jnp.square(means - mean[None]), axis=0
    )
    row = lax.broadcasted_iota(jnp.int32, (8, 128), 0)
    return jnp.where(row == 0, mean, jnp.where(row == 1, squares, 0.0))


def split_piece(total, z):
    tail = total[:, 512 + (z // 2) * 128 : 640 + (z // 2) * 128]
    low = lanes_below_64(SUB)
    if z % 2 == 0:
        packed = jnp.where(low, tail[:SUB], pltpu.roll(tail[SUB:], 64, 1))
    else:
        packed = jnp.where(low, pltpu.roll(tail[:SUB], 64, 1), tail[SUB:])
    return total[:, z * 128 : (z + 1) * 128], packed


def kernel(
    tok_ref, gain_ref, og_ref, w_hbm, act_ref, ng_ref, wg_hbm,
    w, stat_tx, stat_z, stat_y, stat_z_tx, block, gathered, rows, rows_t,
    proj_tx, proj_rx, proj_own, inner, part, ytx, yrx, ztx, zrx, last_tx, last_rx,
    core_tx, core_rx, lo_tx, lo_rx, done,
    w_sem, out_sem, stat_send, stat_recv, perm_send, perm_recv, zg_send, zg_recv,
    yg_send, yg_recv, px_send, px_recv, ix_send, ix_recv, ys_send, ys_recv,
    zs_send, zs_recv, core_send, core_recv, lo_send, lo_recv, fin_send, fin_recv,
):
    r = lax.axis_index("replica")
    x = lax.axis_index("dp")
    m = lax.axis_index("mp")
    y = m // NZ
    z = lax.rem(m, NZ)
    a = y // 2
    b = lax.rem(y, 2)
    y_back = 2 * x + b
    c = lax.rem(r, 2)
    other_core = r + 1 - 2 * c
    other_lo = lax.rem(r + 2, 4)
    moves = a != x

    def at_z(step):
        return lax.rem(z + step, NZ)

    def at_y(step):
        return lax.rem(y + step + NY, NY)

    def at_x(step):
        return lax.rem(x + step, NX)

    barrier = pltpu.get_barrier_semaphore()
    for step in range(1, NZ):
        pl.semaphore_signal(barrier, inc=1, device_id={"mp": y * NZ + at_z(step)}, device_id_type=MESH)
    for step in range(1, NY):
        pl.semaphore_signal(barrier, inc=1, device_id={"mp": at_y(step) * NZ + z}, device_id_type=MESH)
    for step in range(1, NX):
        pl.semaphore_signal(barrier, inc=1, device_id={"dp": at_x(step)}, device_id_type=MESH)
    pl.semaphore_signal(barrier, inc=1, device_id={"replica": other_core}, device_id_type=MESH)
    pl.semaphore_signal(barrier, inc=1, device_id={"replica": other_lo}, device_id_type=MESH)

    @pl.when(moves)
    def _():
        pl.semaphore_signal(barrier, inc=1, device_id={"dp": a, "mp": y_back * NZ + z}, device_id_type=MESH)

    weight_copies = []
    for h in range(2):
        for i, (to, start, size) in enumerate(SEGMENTS):
            weight_copies.append(
                pltpu.make_async_copy(
                    w_hbm.at[pl.ds(h * HALF + start, size), :],
                    w.at[h, pl.ds(to, size), :],
                    w_sem.at[h, i],
                )
            )
    for copy in weight_copies:
        copy.start()

    values = tok_ref[...].astype(F32)
    mean = jnp.mean(values, axis=1, keepdims=True)
    squares = jnp.sum(jnp.square(values - mean), axis=1, keepdims=True)
    lane = lax.broadcasted_iota(jnp.int32, (TOK, 128), 1)
    table = jnp.where(lane == 0, mean, jnp.where(lane == 1, squares, 0.0))
    stats = jnp.transpose(table)[:8, :]
    stat_z_tx[...] = stats
    stat_z[pl.ds(z, 1)] = stats[None]

    pl.semaphore_wait(barrier, 15 + jnp.where(moves, 1, 0))

    copies = []
    for step in range(1, NZ):
        copies.append(
            remote(stat_z_tx, stat_z.at[z], stat_send.at[step], stat_recv.at[z], mp=y * NZ + at_z(step))
        )
        copies[-1].start()
    for step in range(1, NZ):
        remote(
            stat_z_tx, stat_z.at[at_z(step)], stat_send.at[step], stat_recv.at[at_z(step)], mp=y * NZ + at_z(step)
        ).wait_recv()
    stats = merge_stats(stat_z[...], float(FEAT))
    stat_tx[...] = stats
    stat_y[pl.ds(y, 1)] = stats[None]
    for step in range(1, NY):
        copies.append(
            remote(
                stat_tx, stat_y.at[y], stat_send.at[NZ + step], stat_recv.at[NZ + y], mp=at_y(step) * NZ + z
            )
        )
        copies[-1].start()
    for step in range(1, NY):
        remote(
            stat_tx, stat_y.at[at_y(step)], stat_send.at[NZ + step], stat_recv.at[NZ + at_y(step)],
            mp=at_y(step) * NZ + z,
        ).wait_recv()
    stats = merge_stats(stat_y[...], float(HALF))
    table = jnp.transpose(jnp.concatenate([stats, jnp.zeros((120, 128), F32)], axis=0))
    centre = table[:, 0:1]
    scale = lax.rsqrt(table[:, 1:2] * (1.0 / D) + 1e-06)
    normed = (values - centre) * scale * gain_ref[...].astype(F32)
    tail = jnp.concatenate([normed[:, 128:], jnp.zeros((TOK, 64), F32)], axis=1)
    block[0:TOK, :] = normed[:, :128].astype(BF16)
    block[TOK:FEAT, :] = jnp.where(
        lanes_below_64(SUB), tail[:SUB], pltpu.roll(tail[SUB:], 64, 1)
    ).astype(BF16)

    perm = remote(
        block, gathered.at[z], perm_send.at[0], perm_recv.at[0], dp=a, mp=y_back * NZ + z
    )

    @pl.when(moves)
    def _():
        perm.start()
        perm.wait_recv()

    @pl.when(jnp.logical_not(moves))
    def _():
        gathered[pl.ds(z, 1)] = block[...][None]

    for step in range(1, NZ):
        copies.append(
            remote(
                gathered.at[z], gathered.at[z], zg_send.at[step], zg_recv.at[z], mp=y * NZ + at_z(step)
            )
        )
        copies[-1].start()
    for step in range(1, NZ):
        remote(
            gathered.at[at_z(step)], gathered.at[at_z(step)], zg_send.at[step], zg_recv.at[at_z(step)],
            mp=y * NZ + at_z(step),
        ).wait_recv()
    low = lanes_below_64(SUB)
    for zz in range(NZ):
        rows[pl.ds(y, 1), :, zz * 128 : (zz + 1) * 128] = gathered[zz, 0:TOK, :][None]
    for pair in range(NZ // 2):
        first = gathered[2 * pair, TOK:FEAT, :].astype(F32)
        second = gathered[2 * pair + 1, TOK:FEAT, :].astype(F32)
        top = jnp.where(low, first, pltpu.roll(second, 64, 1))
        bottom = jnp.where(low, pltpu.roll(first, 64, 1), second)
        both = jnp.concatenate([top, bottom], axis=0).astype(BF16)
        rows[pl.ds(y, 1), :, 512 + pair * 128 : 640 + pair * 128] = both[None]

    def gather_copy(way, step, sub, source):
        piece = rows.at[source, pl.ds(sub * SUB, SUB), :]
        sign = 1 - 2 * way
        return remote(
            piece, piece, yg_send.at[way, step, sub], yg_recv.at[way, step, sub], mp=at_y(sign) * NZ + z
        )

    def transpose_row(source):
        where_to = pl.multiple_of((source // 2) * TOK, TOK)
        rows_t[pl.ds(lax.rem(source, 2), 1), :, pl.ds(where_to, TOK)] = jnp.transpose(rows[source])[None]

    def project(group, index):
        total = jnp.dot(rows[2 * group], w[0], preferred_element_type=F32) + jnp.dot(
            rows[2 * group + 1], w[1], preferred_element_type=F32
        )

        @pl.when(group == x)
        def _():
            proj_own[...] = total

        @pl.when(group != x)
        def _():
            proj_tx[index] = total.astype(BF16)
            remote(
                proj_tx.at[index], proj_rx.at[x], px_send.at[index], px_recv.at[x], dp=group
            ).start()

    for sub in range(2):
        for way in range(2):
            copies.append(gather_copy(way, 0, sub, y))
            copies[-1].start()
    sign = 1 - 2 * b
    for copy in weight_copies:
        copy.wait()
    transpose_row(y)
    for step in range(1, 5):
        for sub in range(2):
            for way in range(2):
                if step == 4 and sub != way:
                    continue
                source = at_y(-step if way == 0 else step)
                gather_copy(way, step - 1, sub, source).wait_recv()
                if step < 3 or (step == 3 and sub == way):
                    copies.append(gather_copy(way, step, sub, source))
                    copies[-1].start()
        completing = at_y(step * sign if step % 2 else -step * sign)
        project(completing // 2, step - 1)
        transpose_row(at_y(step))
        if step < 4:
            transpose_row(at_y(-step))

    for step in range(1, NX):
        remote(
            proj_tx.at[0], proj_rx.at[at_x(step)], px_send.at[0], px_recv.at[at_x(step)], dp=at_x(step)
        ).wait_recv()
    projected = proj_own[...]
    for step in range(1, NX):
        projected = projected + proj_rx[at_x(step)].astype(F32)
    linear = lax.broadcasted_iota(jnp.int32, (TOK, COLS), 1) < QKV
    normal_cdf = 0.5 * (1.0 + lax.erf(projected * 0.7071067811865476))
    density = jnp.exp(-0.5 * projected * projected) * 0.3989422804014327
    act_ref[...] = jnp.where(linear, projected, projected * normal_cdf).astype(BF16)
    slopes = jnp.where(linear, 1.0, normal_cdf + projected * density)
    inner[pl.ds(x, 1)] = (og_ref[...].astype(F32) * slopes).astype(BF16)[None]

    for step in range(1, NX):
        copies.append(
            remote(inner.at[x], inner.at[x], ix_send.at[step], ix_recv.at[x], dp=at_x(step))
        )
        copies[-1].start()
    for step in range(1, NX):
        remote(
            inner.at[at_x(step)], inner.at[at_x(step)], ix_send.at[step], ix_recv.at[at_x(step)], dp=at_x(step)
        ).wait_recv()
    every = inner[...].reshape(NX * TOK, COLS)

    def weight_piece(half, k):
        left = rows_t[half, k * CHUNK : (k + 1) * CHUNK, :]
        return jnp.dot(left, every, preferred_element_type=F32)

    pieces = HALF // CHUNK

    def core_copy(k):
        return remote(
            core_tx.at[k], core_rx.at[k], core_send.at[k], core_recv.at[k], replica=other_core
        )

    def lo_copy(k):
        return remote(lo_tx.at[k], lo_rx.at[k], lo_send.at[k], lo_recv.at[k], replica=other_lo)

    def done_copy(k, half):
        return remote(
            done.at[half, k], done.at[half, k], fin_send.at[k], fin_recv.at[k], replica=other_core
        )

    for k in range(pieces):
        core_tx[k] = weight_piece(1 - c, k).astype(BF16)
        core_copy(k).start()

    def fill_part(target):
        group, half = target // 2, lax.rem(target, 2)
        part[pl.ds(target, 1)] = lax.dot_general(
            inner[group], w[half], (((1,), (1,)), ((), ())), preferred_element_type=F32
        )[None]

    lax.fori_loop(0, NY, lambda i, carry: (fill_part(i), carry)[1], 0)

    def ring_copy(way, h, sub):
        piece = pl.ds(sub * SUB, SUB)
        sign = 1 - 2 * way
        return remote(
            ytx.at[way, h - 1, piece, :],
            yrx.at[way, h - 1, piece, :],
            ys_send.at[way, h - 1, sub],
            ys_recv.at[way, h - 1, sub],
            mp=at_y(sign) * NZ + z,
        )

    def ring_send(way, h, sub):
        sign = 1 - 2 * way
        piece = slice(sub * SUB, (sub + 1) * SUB)
        value = part[at_y(sign * h), piece, :]
        farthest = 4 if sub == way else 3
        if h < farthest:
            ring_copy(way, h + 1, sub).wait_recv()
            value = value + yrx[way, h, piece, :].astype(F32)
        ytx[way, h - 1, piece, :] = value.astype(BF16)
        copies.append(ring_copy(way, h, sub))
        copies[-1].start()

    ring_send(0, 4, 0)
    ring_send(1, 4, 1)
    ring_send(0, 3, 1)
    ring_send(1, 3, 0)

    def weight_stage(k):
        own = weight_piece(c, k)
        core_copy(k).wait_recv()
        own = own + core_rx[k].astype(F32)
        lo_tx[k] = own.astype(BF16)
        lo_copy(k).start()

    out_copies = []

    def out_copy(half, k, index):
        segments = [
            (i, s) for i, s in enumerate(SEGMENTS) if k * CHUNK <= s[0] < (k + 1) * CHUNK
        ]
        for i, (place, start, size) in segments:
            copy = pltpu.make_async_copy(
                done.at[half, k, pl.ds(place - k * CHUNK, size), :],
                wg_hbm.at[pl.ds(half * HALF + start, size), :],
                out_sem.at[index, i],
            )
            copy.start()
            out_copies.append(copy)

    def finish_stage(k):
        lo_copy(k).wait_recv()
        total = lo_tx[k].astype(F32) + lo_rx[k].astype(F32)
        done[pl.ds(c, 1), k] = (total * 0.25).astype(BF16)[None]
        done_copy(k, c).start()
        out_copy(c, k, 0)

    for k in range(pieces):
        weight_stage(k)
    ring_send(0, 3, 0)
    ring_send(1, 3, 1)
    ring_send(0, 2, 1)
    ring_send(1, 2, 0)
    ring_send(0, 2, 0)
    ring_send(1, 2, 1)
    ring_send(0, 1, 1)
    ring_send(1, 1, 0)
    finish_stage(0)
    ring_send(0, 1, 0)
    ring_send(1, 1, 1)
    finish_stage(1)
    for way, sub in ((0, 1), (1, 0), (0, 0), (1, 1)):
        ring_copy(way, 1, sub).wait_recv()
    total = part[y] + yrx[0, 0].astype(F32) + yrx[1, 0].astype(F32)

    for zz in range(NZ):
        first, packed = split_piece(total, zz)
        ztx[zz, 0:TOK, :] = first.astype(BF16)
        ztx[zz, TOK:FEAT, :] = packed.astype(BF16)
    for step in range(1, NZ):
        copies.append(
            remote(ztx.at[at_z(step)], zrx.at[z], zs_send.at[step], zs_recv.at[z], mp=y * NZ + at_z(step))
        )
        copies[-1].start()
    for step in range(1, NZ):
        remote(
            ztx.at[0], zrx.at[at_z(step)], zs_send.at[step], zs_recv.at[at_z(step)], mp=y * NZ + at_z(step)
        ).wait_recv()
    total = ztx[z].astype(F32)
    for step in range(1, NZ):
        total = total + zrx[at_z(step)].astype(F32)
    last_tx[...] = total.astype(BF16)
    back = remote(
        last_tx, last_rx, perm_send.at[1], perm_recv.at[1], dp=a, mp=y_back * NZ + z
    )

    @pl.when(moves)
    def _():
        back.start()

    finish_stage(2)

    @pl.when(moves)
    def _():
        back.wait_recv()

    @pl.when(jnp.logical_not(moves))
    def _():
        last_rx[...] = last_tx[...]

    ng_ref[:, 0:128] = last_rx[0:TOK, :]
    packed = last_rx[TOK:FEAT, :].astype(F32)
    ng_ref[0:SUB, 128:FEAT] = packed[:, :64].astype(BF16)
    ng_ref[SUB:TOK, 128:FEAT] = pltpu.roll(packed, 64, 1)[:, :64].astype(BF16)

    for k in range(pieces):
        done_copy(k, 1 - c).wait_recv()
        out_copy(1 - c, k, 1)

    @pl.when(moves)
    def _():
        perm.wait_send()
        back.wait_send()

    for index in range(4):
        step = index + 1
        group = at_y(step * sign if step % 2 else -step * sign) // 2

        @pl.when(group != x)
        def _():
            remote(
                proj_tx.at[index], proj_rx.at[x], px_send.at[index], px_recv.at[x], dp=group
            ).wait_send()

    for copy in copies:
        copy.wait_send()
    for k in range(pieces):
        core_copy(k).wait_send()
        lo_copy(k).wait_send()
        done_copy(k, c).wait_send()
    for copy in out_copies:
        copy.wait()


def local(tokens, norm_gain, joined_weight, output_grad):
    start = lax.axis_index("mp") * FEAT
    gain = lax.dynamic_slice(norm_gain, (start,), (FEAT,)).reshape(1, FEAT)
    vmem = pl.BlockSpec(memory_space=pltpu.VMEM)
    anywhere = pl.BlockSpec(memory_space=pl.ANY)
    dma = pltpu.SemaphoreType.DMA
    pieces = HALF // CHUNK
    scratch = [
        pltpu.VMEM((2, HALF, COLS), BF16),
        pltpu.VMEM((8, 128), F32),
        pltpu.VMEM((NZ, 8, 128), F32),
        pltpu.VMEM((NY, 8, 128), F32),
        pltpu.VMEM((8, 128), F32),
        pltpu.VMEM((FEAT, 128), BF16),
        pltpu.VMEM((NZ, FEAT, 128), BF16),
        pltpu.VMEM((NY, TOK, HALF), BF16),
        pltpu.VMEM((2, HALF, NX * TOK), BF16),
        pltpu.VMEM((NX, TOK, COLS), BF16),
        pltpu.VMEM((NX, TOK, COLS), BF16),
        pltpu.VMEM((TOK, COLS), F32),
        pltpu.VMEM((NX, TOK, COLS), BF16),
        pltpu.VMEM((NY, TOK, HALF), F32),
        pltpu.VMEM((2, 4, TOK, HALF), BF16),
        pltpu.VMEM((2, 4, TOK, HALF), BF16),
        pltpu.VMEM((NZ, FEAT, 128), BF16),
        pltpu.VMEM((NZ, FEAT, 128), BF16),
        pltpu.VMEM((FEAT, 128), BF16),
        pltpu.VMEM((FEAT, 128), BF16),
        pltpu.VMEM((pieces, CHUNK, COLS), BF16),
        pltpu.VMEM((pieces, CHUNK, COLS), BF16),
        pltpu.VMEM((pieces, CHUNK, COLS), BF16),
        pltpu.VMEM((pieces, CHUNK, COLS), BF16),
        pltpu.VMEM((2, pieces, CHUNK, COLS), BF16),
        dma((2, 8)),
        dma((2, 8)),
        dma((NZ + NY,)),
        dma((NZ + NY,)),
        dma((2,)),
        dma((2,)),
        dma((NZ,)),
        dma((NZ,)),
        dma((2, 4, 2)),
        dma((2, 4, 2)),
        dma((NX,)),
        dma((NX,)),
        dma((NX,)),
        dma((NX,)),
        dma((2, 4, 2)),
        dma((2, 4, 2)),
        dma((NZ,)),
        dma((NZ,)),
        dma((pieces,)),
        dma((pieces,)),
        dma((pieces,)),
        dma((pieces,)),
        dma((pieces,)),
        dma((pieces,)),
    ]
    return pl.pallas_call(
        kernel,
        out_shape=(
            jax.ShapeDtypeStruct((TOK, COLS), BF16),
            jax.ShapeDtypeStruct((TOK, FEAT), BF16),
            jax.ShapeDtypeStruct((2 * HALF, COLS), BF16),
        ),
        in_specs=[vmem, vmem, vmem, anywhere],
        out_specs=(vmem, vmem, anywhere),
        scratch_shapes=scratch,
        compiler_params=pltpu.CompilerParams(
            collective_id=0, has_side_effects=True, vmem_limit_bytes=56 * 1024 * 1024
        ),
        cost_estimate=pl.CostEstimate(flops=3200000000, bytes_accessed=5000000, transcendentals=200000),
    )(tokens, gain, output_grad, joined_weight)


def solution(mesh):
    in_specs = (P(("replica", "dp"), "mp"), P(), P("dp", "mp"), P(("replica", "dp"), "mp"))
    out_specs = (P(("replica", "dp"), "mp"), P(("replica", "dp"), "mp"), P("dp", "mp"))
    return jax.shard_map(local, mesh=mesh, in_specs=in_specs, out_specs=out_specs, check_vma=False)
```

time: 524 us -> 133 us (0.25)
  the two profiles are of different devices: /device:TPU:1 before, /device:TPU:6 now
where the time goes in v1:
time: 133 us; the launch traced here: 132 us
  Pallas kernels  116 us (87%)
  local copies, waits for them, and re-layouts  16.2 us (12%)
    pallas_call x1, Pallas kernels, local(): pl.pallas_call(kernel, out_shape=(jax.ShapeDtypeStruct((TOK, COLS), BF16)...  116 us
    unnamed x3, local copies, waits for them, and re-layouts  7.42 us
    pallas_call x3, local copies, waits for them, and re-layouts, local(): pl.pallas_call(kernel, out_shape=(jax.ShapeDtypeStruct((TOK, COLS), BF16)...  7.41 us

profile of v1, /device:TPU:6, one launch (start us, length us, event | category | flops | bytes accessed | tf_op | source)
XLA Modules:
  0.0 132.4 jit_solution(6918228854807862640)
XLA Ops:
  0.6 0.8 dynamic_slice.3
  1.4 0.6 reshape.9.gain_ref
  2.0 1.5 %copy.7.tok_ref = bf16[128,192]{1,0:T(8,128)(2,1)} copy(bf16[128,192]{0,1:T(8,128)(2,1)} %param.4) | data formatting | bytes 98304 | tf_op args[0]
  3.5 1.7 %copy.8.og_ref = bf16[128,672]{1,0:T(8,128)(2,1)} copy(bf16[128,672]{0,1:T(8,128)(2,1)} %param.7) | data formatting | bytes 344064 | tf_op args[3]
  5.2 4.2 %copy.9.w_hbm = bf16[1536,672]{1,0:T(8,128)(2,1)} copy(bf16[1536,672]{0,1:T(8,128)(2,1)} %param.6) | data formatting | bytes 4128768 | tf_op args[2]
  9.4 115.5 %shard_map.67 = (bf16[128,672]{1,0:T(8,128)(2,1)}, bf16[128,192]{1,0:T(8,128)(2,1)}, bf16[1536,672]{1,0:T(8,128)(2,1)}) custom-call(bf16[128,192]{1,0:T(8,128)(2,1)} %copy.7.tok_ref, bf16[1,192]{1,0:T(2,128)(2,1)} %reshape.9.gain_ref, bf16[128,672]{1,0:T(8,128)(2,1)} %copy.8.og_ref, bf16[1536,672]{1,0:T(8,128)(2,1)} %copy.9.w_hbm), custom_call_target="tpu_custom_call" | custom-call | flops 3200000000 | bytes 5000000 | tf_op jit(solution)/shard_map/pallas_call | solution.py:517
  124.9 1.7 %copy.10 = bf16[128,672]{0,1:T(8,128)(2,1)} copy(bf16[128,672]{1,0:T(8,128)(2,1)} %get-tuple-element.3) | data formatting | bytes 344064 | tf_op jit(solution)/shard_map/pallas_call | solution.py:517
  126.7 1.6 %copy.11 = bf16[128,192]{0,1:T(8,128)(2,1)} copy(bf16[128,192]{1,0:T(8,128)(2,1)} %get-tuple-element.4) | data formatting | bytes 98304 | tf_op jit(solution)/shard_map/pallas_call | solution.py:517
  128.2 4.1 %copy.12 = bf16[1536,672]{0,1:T(8,128)(2,1)} copy(bf16[1536,672]{1,0:T(8,128)(2,1)} %get-tuple-element.5) | data formatting | bytes 4128768 | tf_op jit(solution)/shard_map/pallas_call | solution.py:517

commit v2 on v0

v2 whole, which is shorter than its diff:
```python
import jax
import jax.numpy as jnp
from jax import lax
from jax.experimental import pallas as pl
from jax.experimental.pallas import tpu as pltpu
from jax.sharding import PartitionSpec as P

MESH = pl.DeviceIdType.MESH
F32 = jnp.float32
BF16 = jnp.bfloat16

NX = 4
NY = 8
NZ = 4
TOK = 128
FEAT = 192
HALF = NZ * FEAT
COLS = 672
QKV = 288
D = 6144
CHUNK = 256
PIECES = HALF // CHUNK


def remote(src, dst, send_sem, recv_sem, **device):
    return pltpu.make_async_remote_copy(
        src_ref=src,
        dst_ref=dst,
        send_sem=send_sem,
        recv_sem=recv_sem,
        device_id=device,
        device_id_type=MESH,
    )


def merge_stats(stack, features):
    count = stack.shape[0]
    means = stack[:, 0:1, :]
    mean = jnp.sum(means, axis=0) / count
    squares = jnp.sum(stack[:, 1:2, :], axis=0) + features * jnp.sum(
        jnp.square(means - mean[None]), axis=0
    )
    return stats_table(mean, squares)


def stats_table(mean, squares):
    row = lax.broadcasted_iota(jnp.int32, (8, 128), 0)
    return jnp.where(row == 0, mean, jnp.where(row == 1, squares, 0.0))


def kernel(
    tok_ref, gain_ref, og_hbm, w_hbm, act_ref, ng_ref, wg_hbm,
    w, w_turned, og, gain_rows, gain, stat_z_tx, stat_y_tx, stat_z, stat_y, stat_x, rows, normed,
    site_rows, proj_tx, proj_rx, proj_own, inner, part, ytx, yrx, ztx, zrx, last_tx,
    w_sum, done,
    w_sem, out_sem, stat_send, stat_recv, perm_send, perm_recv, zg_send, zg_recv,
    yg_send, yg_recv, site_send, site_recv, px_send, px_recv, ix_send, lo_send, core_send, inner_recv,
    ys_send, ys_recv, zs_send, zs_recv, fin_send, fin_recv,
):
    r = lax.axis_index("replica")
    x = lax.axis_index("dp")
    m = lax.axis_index("mp")
    y = m // NZ
    z = lax.rem(m, NZ)
    a = y // 2
    b = lax.rem(y, 2)
    y_back = 2 * x + b
    c = lax.rem(r, 2)
    other_core = r + 1 - 2 * c
    other_lo = lax.rem(r + 2, 4)
    across = 3 - r
    moves = a != x

    def at_z(step):
        return lax.rem(z + step, NZ)

    def at_y(step):
        return lax.rem(y + step + NY, NY)

    def at_x(step):
        return lax.rem(x + step, NX)

    def mp(y_place, z_place):
        return y_place * NZ + z_place

    copies = []

    def start(copy):
        copies.append(copy)
        copy.start()

    barrier = pltpu.get_barrier_semaphore()
    greeted = [{"mp": mp(y, at_z(step))} for step in range(1, NZ)]
    greeted += [{"mp": mp(at_y(step), z)} for step in range(1, NY)]
    greeted += [{"dp": at_x(step)} for step in range(1, NX)]
    greeted += [{"replica": other_core}, {"replica": other_lo}, {"replica": across}]
    for device in greeted:
        pl.semaphore_signal(barrier, inc=1, device_id=device, device_id_type=MESH)

    @pl.when(moves)
    def _():
        pl.semaphore_signal(
            barrier, inc=1, device_id={"dp": a, "mp": mp(y_back, z)}, device_id_type=MESH
        )

    w_copy = pltpu.make_async_copy(w_hbm, w, w_sem.at[0])
    og_copy = pltpu.make_async_copy(og_hbm, og, w_sem.at[1])
    w_copy.start()
    og_copy.start()

    values = tok_ref[...].astype(F32)
    mean = jnp.mean(values, axis=0, keepdims=True)
    squares = jnp.sum(jnp.square(values - mean), axis=0, keepdims=True)
    stats = stats_table(mean, squares)
    stat_z_tx[...] = stats
    stat_z[pl.ds(z, 1)] = stats[None]

    pl.semaphore_wait(barrier, len(greeted) + jnp.where(moves, 1, 0))

    def z_block(source_y, source_z):
        return rows.at[source_y, pl.ds(pl.multiple_of(source_z * FEAT, FEAT), FEAT), :]

    def perm_copy():
        return remote(
            tok_ref, z_block(y_back, z), perm_send.at[0], perm_recv.at[0], dp=a, mp=mp(y_back, z)
        )

    def back_copy():
        return remote(
            last_tx, ng_ref, perm_send.at[1], perm_recv.at[1], dp=a, mp=mp(y_back, z)
        )

    def stat_z_copy(step, slot):
        return remote(
            stat_z_tx, stat_z.at[slot], stat_send.at[step], stat_recv.at[slot], mp=mp(y, at_z(step))
        )

    def stat_y_copy(step, slot):
        return remote(
            stat_y_tx, stat_y.at[slot], stat_send.at[NZ + step], stat_recv.at[NZ + slot],
            mp=mp(at_y(step), z),
        )

    def stat_x_copy(step, slot):
        return remote(
            stat_x.at[slot], stat_x.at[slot], stat_send.at[NZ + NY + step],
            stat_recv.at[NZ + NY + slot], dp=at_x(step),
        )

    @pl.when(moves)
    def _():
        perm_copy().start()

    for step in range(1, NZ):
        start(stat_z_copy(step, z))

    @pl.when(jnp.logical_not(moves))
    def _():
        rows[pl.ds(y, 1), pl.ds(pl.multiple_of(z * FEAT, FEAT), FEAT), :] = tok_ref[...][None]

    gain_rows[...] = gain_ref[...].astype(F32)
    table = jnp.transpose(
        jnp.concatenate([gain_rows[pl.ds(12 * x, 12), :], jnp.zeros((116, 128), F32)], axis=0)
    )
    for i in range(12):
        gain[i * 128 : (i + 1) * 128, :] = jnp.broadcast_to(table[:, i : i + 1], (128, 128))

    for step in range(1, NZ):
        stat_z_copy(step, at_z(step)).wait_recv()
    stats = merge_stats(stat_z[...], float(FEAT))
    stat_y_tx[...] = stats
    stat_y[pl.ds(y, 1)] = stats[None]
    for step in range(1, NY):
        start(stat_y_copy(step, y))

    @pl.when(moves)
    def _():
        perm_copy().wait_recv()


    def gather_z(step, source):
        piece = z_block(y, source)
        return remote(piece, piece, zg_send.at[step], zg_recv.at[source], mp=mp(y, at_z(step)))

    def gather_y(way, step, k, source):
        piece = z_block(source, at_z(k))
        return remote(
            piece, piece, yg_send.at[way, step, k], yg_recv.at[way, step, k],
            mp=mp(at_y(1 - 2 * way), z),
        )

    for step in range(1, NZ):
        start(gather_z(step, z))
    for way in range(2):
        start(gather_y(way, 0, 0, y))
    for step in range(1, NY):
        stat_y_copy(step, at_y(step)).wait_recv()
    stat_x[pl.ds(x, 1)] = merge_stats(stat_y[...], float(HALF))[None]
    for step in range(1, NX):
        start(stat_x_copy(step, x))
    for k in range(1, NZ):
        gather_z(k, at_z(k)).wait_recv()
        for way in range(2):
            start(gather_y(way, 0, k, y))
    w_copy.wait()

    def turn(piece):
        columns = slice(piece * HALF // 2, (piece + 1) * HALF // 2)
        w_turned[columns, :] = jnp.transpose(w[:, columns])

    turn(0)
    for step in range(1, NX):
        stat_x_copy(step, at_x(step)).wait_recv()

    def site_copy(t, replica):
        return remote(
            normed.at[t], site_rows.at[r, t // 2], site_send.at[replica // 2, t],
            site_recv.at[r, t // 2], replica=replica,
        )

    def normalize(t):
        h = lax.rem(t, 2)
        statistics = stat_x[t // 2]
        scale = lax.rsqrt(statistics[1:2] * (1.0 / D) + 1e-06)
        column = gain[pl.ds(pl.multiple_of(h * HALF, HALF), HALF), :]
        value = (rows[t].astype(F32) - statistics[0:1]) * scale * column
        normed[pl.ds(t, 1)] = value.astype(BF16)[None]
        start(site_copy(t, 2 * (1 - r // 2) + h))

        @pl.when(h != c)
        def _():
            site_copy(t, other_core).start()

    def project(group, index):
        total = jnp.dot(w[:, :HALF], normed[2 * group], preferred_element_type=F32) + jnp.dot(
            w[:, HALF:], normed[2 * group + 1], preferred_element_type=F32
        )

        @pl.when(group == x)
        def _():
            proj_own[...] = total

        @pl.when(group != x)
        def _():
            proj_tx[index] = total.astype(BF16)
            proj_copy(group, index).start()

    def proj_copy(group, index):
        return remote(
            proj_tx.at[index], proj_rx.at[x], px_send.at[index], px_recv.at[x], dp=group
        )

    sign = 1 - 2 * b

    def completed(step):
        return at_y(step * sign if step % 2 else -step * sign) // 2

    normalize(y)
    for step in range(1, 5):
        for k in range(NZ):
            for way in range(2):
                if step == 4 and k % 2 != way:
                    continue
                source = at_y(-step if way == 0 else step)
                gather_y(way, step - 1, k, source).wait_recv()
                if step < 3 or (step == 3 and k % 2 == way):
                    start(gather_y(way, step, k, source))
        normalize(at_y(step))
        if step < 4:
            normalize(at_y(-step))
        project(completed(step), step - 1)
        if step < 4:
            turn(step)

    for step in range(1, NX):
        remote(
            proj_tx.at[0], proj_rx.at[at_x(step)], px_send.at[0], px_recv.at[at_x(step)], dp=at_x(step)
        ).wait_recv()
    projected = proj_own[...]
    for step in range(1, NX):
        projected = projected + proj_rx[at_x(step)].astype(F32)
    og_copy.wait()
    act_ref[0:QKV, :] = projected[0:QKV].astype(BF16)
    inner[pl.ds(r, 1), pl.ds(x, 1), 0:QKV, :] = og[0:QKV, :][None, None]
    hidden = projected[QKV:]
    normal_cdf = 0.5 * (1.0 + lax.erf(hidden * 0.7071067811865476))
    density = jnp.exp(-0.5 * hidden * hidden) * 0.3989422804014327
    act_ref[QKV:, :] = (hidden * normal_cdf).astype(BF16)
    inner[pl.ds(r, 1), pl.ds(x, 1), QKV:, :] = (
        og[QKV:, :].astype(F32) * (normal_cdf + hidden * density)
    ).astype(BF16)[None, None]

    def inner_x(step, source):
        piece = inner.at[r, source]
        return remote(piece, piece, ix_send.at[step], inner_recv.at[r, source], dp=at_x(step))

    def inner_lo(replica, group):
        piece = inner.at[replica, group]
        return remote(
            piece, piece, lo_send.at[group], inner_recv.at[replica, group], replica=other_lo
        )

    def inner_core(replica, group):
        piece = inner.at[replica, group]
        return remote(
            piece, piece, core_send.at[replica // 2, group], inner_recv.at[replica, group],
            replica=other_core,
        )

    for step in range(1, NX):
        start(inner_x(step, x))
    start(inner_lo(r, x))
    start(inner_core(r, x))
    for step in (1, 3, 2):
        inner_x(step, at_x(step)).wait_recv()
        start(inner_lo(r, at_x(step)))
        start(inner_core(r, at_x(step)))

    def every(replica):
        return jnp.concatenate([inner[replica, g] for g in range(NX)], axis=1)


    part[...] = jnp.dot(w_turned[...], every(r), preferred_element_type=F32)

    def part_of(target, k):
        start_row = pl.multiple_of(lax.rem(target, 2) * HALF + at_z(k) * FEAT, FEAT)
        lane = pl.multiple_of((target // 2) * TOK, TOK)
        return part[pl.ds(start_row, FEAT), pl.ds(lane, TOK)]

    def ring_copy(way, h, k):
        return remote(
            ytx.at[way, h - 1, k],
            yrx.at[way, h - 1, k],
            ys_send.at[way, h - 1, k],
            ys_recv.at[way, h - 1, k],
            mp=mp(at_y(1 - 2 * way), z),
        )

    def ring_send(way, h, k):
        value = part_of(at_y((1 - 2 * way) * h), k)
        if h < (4 if k % 2 == way else 3):
            ring_copy(way, h + 1, k).wait_recv()
            value = value + yrx[way, h, k].astype(F32)
        ytx[way, h - 1, k] = value.astype(BF16)
        start(ring_copy(way, h, k))

    def ring_round(h, ks):
        for k in ks:
            for way in range(2):
                if h < 4 or k % 2 == way:
                    ring_send(way, h, k)

    def rows_of(replica, piece):
        return jnp.concatenate([site_rows[replica, g, piece, :] for g in range(NX)], axis=1)

    def own_rows(piece):
        return jnp.concatenate([normed[2 * g + c, piece, :] for g in range(NX)], axis=1)

    def weight_piece(left, right):
        return lax.dot_general(left, right, (((1,), (1,)), ((), ())), preferred_element_type=F32)

    def add_weight(replica):
        for g in range(NX):
            remote(
                normed.at[0], site_rows.at[replica, g], site_send.at[0, 0], site_recv.at[replica, g],
                replica=other_core,
            ).wait_recv()
        left = every(replica)
        for k in range(PIECES):
            piece = slice(k * CHUNK, (k + 1) * CHUNK)
            w_sum[k] += weight_piece(left, rows_of(replica, piece))

    def wait_inner(replica):
        for g in range(NX):
            inner_core(replica, g).wait_recv()

    def pass_on(step):
        inner_lo(other_lo, at_x(step)).wait_recv()
        start(inner_core(other_lo, at_x(step)))

    def done_copy(k, half):
        return remote(
            done.at[half, k], done.at[half, k], fin_send.at[k], fin_recv.at[k], replica=other_core
        )

    out_copies = []

    def out_copy(half, k, index):
        copy = pltpu.make_async_copy(
            done.at[half, k],
            wg_hbm.at[:, pl.ds(pl.multiple_of(half * HALF + k * CHUNK, CHUNK), CHUNK)],
            out_sem.at[index, k],
        )
        copy.start()
        out_copies.append(copy)

    order = (1, 3, 2, 0)
    ring_round(4, order)
    for k in order:
        for way in range(2):
            if k % 2 != way:
                ring_send(way, 3, k)
    for k in range(PIECES):
        w_sum[k] = weight_piece(every(r), own_rows(slice(k * CHUNK, (k + 1) * CHUNK)))
    pass_on(0)
    for k in order:
        for way in range(2):
            if k % 2 == way:
                ring_send(way, 3, k)
    wait_inner(other_core)
    add_weight(other_core)
    ring_round(2, order[:2])
    pass_on(1)
    ring_round(2, order[2:])
    pass_on(3)
    ring_round(1, order[:2])
    pass_on(2)
    ring_round(1, order[2:])
    add_weight(other_lo)

    def scatter_z(step, source):
        return remote(
            ztx.at[step], zrx.at[source], zs_send.at[step], zs_recv.at[source], mp=mp(y, at_z(step))
        )

    for k in order:
        for way in range(2):
            ring_copy(way, 1, k).wait_recv()
        total = part_of(y, k) + yrx[0, 0, k].astype(F32) + yrx[1, 0, k].astype(F32)
        if k:
            ztx[k] = total.astype(BF16)
            start(scatter_z(k, z))
    wait_inner(across)
    add_weight(across)
    for step in range(1, NZ):
        scatter_z(step, at_z(step)).wait_recv()
        total = total + zrx[at_z(step)].astype(F32)

    @pl.when(moves)
    def _():
        last_tx[...] = total.astype(BF16)
        back_copy().start()

    @pl.when(jnp.logical_not(moves))
    def _():
        ng_ref[...] = total.astype(BF16)

    for k in range(PIECES):
        done[pl.ds(c, 1), k] = (w_sum[k] * 0.25).astype(BF16)[None]
        start(done_copy(k, c))
        out_copy(c, k, 0)
    for k in range(PIECES):
        done_copy(k, 1 - c).wait_recv()
        out_copy(1 - c, k, 1)

    @pl.when(moves)
    def _():
        back_copy().wait_recv()
        back_copy().wait_send()
        perm_copy().wait_send()

    for index in range(NX):
        @pl.when(completed(index + 1) != x)
        def _(index=index):
            proj_copy(completed(index + 1), index).wait_send()

    for g in range(NX):
        site_copy(2 * g + 1 - c, other_core).wait_send()
    for copy in copies:
        copy.wait_send()
    for copy in out_copies:
        copy.wait()


def hand_over(act_in, ng_in, wg_in, act_out, ng_out, wg_out, act, ng, wg, sem):
    pieces = [(act_in, act, act_out), (ng_in, ng, ng_out)]
    for i in range(6):
        piece = pl.ds(i * 112, 112)
        pieces.append((wg_in.at[piece, :], wg.at[piece, :], wg_out.at[piece, :]))
    loads = [
        pltpu.make_async_copy(source, held, sem.at[0, i]) for i, (source, held, _) in enumerate(pieces)
    ]
    stores = [
        pltpu.make_async_copy(held, target, sem.at[1, i]) for i, (_, held, target) in enumerate(pieces)
    ]
    for load in loads:
        load.start()
    for load, store in zip(loads, stores):
        load.wait()
        store.start()
    for store in stores:
        store.wait()


def local(tokens, norm_gain, joined_weight, output_grad):
    vmem = pl.BlockSpec(memory_space=pltpu.VMEM)
    anywhere = pl.BlockSpec(memory_space=pl.ANY)
    dma = pltpu.SemaphoreType.DMA
    scratch = [
        pltpu.VMEM((COLS, 2 * HALF), BF16),
        pltpu.VMEM((2 * HALF, COLS), BF16),
        pltpu.VMEM((COLS, TOK), BF16),
        pltpu.VMEM((D // 128, 128), F32),
        pltpu.VMEM((2 * HALF, TOK), F32),
        pltpu.VMEM((8, 128), F32),
        pltpu.VMEM((8, 128), F32),
        pltpu.VMEM((NZ, 8, 128), F32),
        pltpu.VMEM((NY, 8, 128), F32),
        pltpu.VMEM((NX, 8, 128), F32),
        pltpu.VMEM((NY, HALF, TOK), BF16),
        pltpu.VMEM((NY, HALF, TOK), BF16),
        pltpu.VMEM((4, NX, HALF, TOK), BF16),
        pltpu.VMEM((NX, COLS, TOK), BF16),
        pltpu.VMEM((NX, COLS, TOK), BF16),
        pltpu.VMEM((COLS, TOK), F32),
        pltpu.VMEM((4, NX, COLS, TOK), BF16),
        pltpu.VMEM((2 * HALF, NX * TOK), F32),
        pltpu.VMEM((2, 4, NZ, FEAT, TOK), BF16),
        pltpu.VMEM((2, 4, NZ, FEAT, TOK), BF16),
        pltpu.VMEM((NZ, FEAT, TOK), BF16),
        pltpu.VMEM((NZ, FEAT, TOK), BF16),
        pltpu.VMEM((FEAT, TOK), BF16),
        pltpu.VMEM((PIECES, COLS, CHUNK), F32),
        pltpu.VMEM((2, PIECES, COLS, CHUNK), BF16),
        dma((2,)),
        dma((2, PIECES)),
        dma((NZ + NY + NX,)),
        dma((NZ + NY + NX,)),
        dma((2,)),
        dma((2,)),
        dma((NZ,)),
        dma((NZ,)),
        dma((2, 4, NZ)),
        dma((2, 4, NZ)),
        dma((2, NY)),
        dma((4, NX)),
        dma((NX,)),
        dma((NX,)),
        dma((NX,)),
        dma((NX,)),
        dma((2, NX)),
        dma((4, NX)),
        dma((2, 4, NZ)),
        dma((2, 4, NZ)),
        dma((NZ,)),
        dma((NZ,)),
        dma((PIECES,)),
        dma((PIECES,)),
    ]
    shapes = (
        jax.ShapeDtypeStruct((COLS, TOK), BF16),
        jax.ShapeDtypeStruct((FEAT, TOK), BF16),
        jax.ShapeDtypeStruct((COLS, 2 * HALF), BF16),
    )
    results = pl.pallas_call(
        kernel,
        out_shape=shapes,
        in_specs=[vmem, vmem, anywhere, anywhere],
        out_specs=(vmem, vmem, anywhere),
        scratch_shapes=scratch,
        compiler_params=pltpu.CompilerParams(
            collective_id=0, has_side_effects=True, vmem_limit_bytes=56 * 1024 * 1024
        ),
        cost_estimate=pl.CostEstimate(flops=3200000000, bytes_accessed=5000000, transcendentals=200000),
    )(
        tokens.T,
        norm_gain.reshape(D // 128, 128),
        output_grad.T,
        joined_weight.T,
    )
    activated, normed_grad, weight_grad = pl.pallas_call(
        hand_over,
        out_shape=shapes,
        in_specs=[anywhere] * 3,
        out_specs=(anywhere,) * 3,
        scratch_shapes=[pltpu.VMEM(shape.shape, BF16) for shape in shapes] + [dma((2, 8))],
        cost_estimate=pl.CostEstimate(flops=0, bytes_accessed=4600000, transcendentals=0),
    )(*results)
    return activated.T, normed_grad.T, weight_grad.T


def solution(mesh):
    in_specs = (P(("replica", "dp"), "mp"), P(), P("dp", "mp"), P(("replica", "dp"), "mp"))
    out_specs = (P(("replica", "dp"), "mp"), P(("replica", "dp"), "mp"), P("dp", "mp"))
    return jax.shard_map(local, mesh=mesh, in_specs=in_specs, out_specs=out_specs, check_vma=False)
```

time: 524 us -> 98 us (0.19)
  the two profiles are of different devices: /device:TPU:1 before, /device:TPU:4 now
where the time goes in v2:
time: 98 us; the launch traced here: 97.8 us
  Pallas kernels  97.1 us (99%)
    pallas_call x1, Pallas kernels, local(): pl.pallas_call(kernel, out_shape=shapes, in_specs=[vmem, vmem, anywhere,...  94.6 us
    pallas_call x1, Pallas kernels, local(): pl.pallas_call(hand_over, out_shape=shapes, in_specs=[anywhere] * 3, out_...  2.54 us

profile of v2, /device:TPU:4, one launch (start us, length us, event | category | flops | bytes accessed | tf_op | source)
XLA Modules:
  0.0 97.8 jit_solution(12724679599049080997)
XLA Ops:
  0.6 94.6 %shard_map.67 = (bf16[672,128]{1,0:T(8,128)(2,1)}, bf16[192,128]{1,0:T(8,128)(2,1)}, bf16[672,1536]{1,0:T(8,128)(2,1)}) custom-call(bf16[192,128]{1,0:T(8,128)(2,1)} %bitcast.11, bf16[48,128]{1,0:T(8,128)(2,1)} %bitcast.13, bf16[672,128]{1,0:T(8,128)(2,1)} %bitcast.9, bf16[672,1536]{1,0:T(8,128)(2,1)} %bitcast.7), custom_call_target="tpu_custom_call" | custom-call | flops 3200000000 | bytes 5000000 | tf_op jit(solution)/shard_map/pallas_call | solution.py:555
  95.2 2.5 %shard_map.68 = (bf16[672,128]{1,0:T(8,128)(2,1)}, bf16[192,128]{1,0:T(8,128)(2,1)}, bf16[672,1536]{1,0:T(8,128)(2,1)}) custom-call(bf16[672,128]{1,0:T(8,128)(2,1)} %get-tuple-element.9.act_in, bf16[192,128]{1,0:T(8,128)(2,1)} %get-tuple-element.10.ng_in, bf16[672,1536]{1,0:T(8,128)(2,1)} %get-tuple-element.11.wg_in), custom_call_target="tpu_custom_call" | custom-call | bytes 4600000 | tf_op jit(solution)/shard_map/pallas_call | solution.py:571

commit v3 on v2

--- a/solution.py
+++ b/solution.py
@@ -20,6 +20,9 @@
 D = 6144
 CHUNK = 256
 PIECES = HALF // CHUNK
+FAR = 2
+PARTS = 3
+PART = COLS // PARTS
 
 
 def remote(src, dst, send_sem, recv_sem, **device):
@@ -52,10 +55,10 @@
     tok_ref, gain_ref, og_hbm, w_hbm, act_ref, ng_ref, wg_hbm,
     w, w_turned, og, gain_rows, gain, stat_z_tx, stat_y_tx, stat_z, stat_y, stat_x, rows, normed,
     site_rows, proj_tx, proj_rx, proj_own, inner, part, ytx, yrx, ztx, zrx, last_tx,
-    w_sum, done,
+    w_sum, w_far, lo_tx, lo_rx, done,
     w_sem, out_sem, stat_send, stat_recv, perm_send, perm_recv, zg_send, zg_recv,
-    yg_send, yg_recv, site_send, site_recv, px_send, px_recv, ix_send, lo_send, core_send, inner_recv,
-    ys_send, ys_recv, zs_send, zs_recv, fin_send, fin_recv,
+    yg_send, yg_recv, site_send, site_recv, px_send, px_recv, ix_send, ix_recv, lo_send, core_send, inner_recv,
+    ys_send, ys_recv, zs_send, zs_recv, sum_send, sum_recv, fin_send, fin_recv,
 ):
     r = lax.axis_index("replica")
     x = lax.axis_index("dp")
@@ -65,6 +68,8 @@
     a = y // 2
     b = lax.rem(y, 2)
     y_back = 2 * x + b
+    back_x = lax.rem(a + 2, NX)
+    from_y = 2 * lax.rem(x + 2, NX) + b
     c = lax.rem(r, 2)
     other_core = r + 1 - 2 * c
     other_lo = lax.rem(r + 2, 4)
@@ -94,6 +99,7 @@
     greeted += [{"mp": mp(at_y(step), z)} for step in range(1, NY)]
     greeted += [{"dp": at_x(step)} for step in range(1, NX)]
     greeted += [{"replica": other_core}, {"replica": other_lo}, {"replica": across}]
+    greeted += [{"dp": a, "mp": mp(from_y, z)}]
     for device in greeted:
         pl.semaphore_signal(barrier, inc=1, device_id=device, device_id_type=MESH)
 
@@ -123,11 +129,6 @@
     def perm_copy():
         return remote(
             tok_ref, z_block(y_back, z), perm_send.at[0], perm_recv.at[0], dp=a, mp=mp(y_back, z)
-        )
-
-    def back_copy():
-        return remote(
-            last_tx, ng_ref, perm_send.at[1], perm_recv.at[1], dp=a, mp=mp(y_back, z)
         )
 
     def stat_z_copy(step, slot):
@@ -212,10 +213,11 @@
     for step in range(1, NX):
         stat_x_copy(step, at_x(step)).wait_recv()
 
-    def site_copy(t, replica):
-        return remote(
-            normed.at[t], site_rows.at[r, t // 2], site_send.at[replica // 2, t],
-            site_recv.at[r, t // 2], replica=replica,
+    def site_copy(source, t, replica, features):
+        piece = pl.ds(0, features)
+        return remote(
+            normed.at[t, piece, :], site_rows.at[source, t // 2, piece, :],
+            site_send.at[replica // 2, t], site_recv.at[source, t // 2], replica=replica,
         )
 
     def normalize(t):
@@ -225,30 +227,75 @@
         column = gain[pl.ds(pl.multiple_of(h * HALF, HALF), HALF), :]
         value = (rows[t].astype(F32) - statistics[0:1]) * scale * column
         normed[pl.ds(t, 1)] = value.astype(BF16)[None]
-        start(site_copy(t, 2 * (1 - r // 2) + h))
+        start(site_copy(r, t, 2 * (1 - r // 2) + h, FAR * CHUNK))
 
         @pl.when(h != c)
         def _():
-            site_copy(t, other_core).start()
+            site_copy(r, t, other_core, HALF).start()
 
     def project(group, index):
-        total = jnp.dot(w[:, :HALF], normed[2 * group], preferred_element_type=F32) + jnp.dot(
-            w[:, HALF:], normed[2 * group + 1], preferred_element_type=F32
-        )
-
-        @pl.when(group == x)
+        for i in range(PARTS):
+            columns = slice(i * PART, (i + 1) * PART)
+            total = jnp.dot(
+                w[columns, :HALF], normed[2 * group], preferred_element_type=F32
+            ) + jnp.dot(w[columns, HALF:], normed[2 * group + 1], preferred_element_type=F32)
+
+            @pl.when(group == x)
+            def _(columns=columns, total=total):
+                proj_own[columns, :] = total
+
+            @pl.when(group != x)
+            def _(i=i, columns=columns, total=total):
+                proj_tx[index, columns, :] = total.astype(BF16)
+                proj_copy(group, index, i).start()
+
+    def proj_copy(group, index, i):
+        columns = pl.ds(i * PART, PART)
+        return remote(
+            proj_tx.at[index, columns, :], proj_rx.at[x, columns, :],
+            px_send.at[index, i], px_recv.at[x, i], dp=group,
+        )
+
+    def proj_wait(source, i):
+        columns = pl.ds(i * PART, PART)
+        remote(
+            proj_tx.at[0, columns, :], proj_rx.at[source, columns, :],
+            px_send.at[0, i], px_recv.at[source, i], dp=source,
+        ).wait_recv()
+
+    def activate_rows(low, high):
+        columns = slice(low, high)
+        projected = proj_own[columns, :]
+        for step in range(1, NX):
+            projected = projected + proj_rx[at_x(step), columns, :].astype(F32)
+        if high <= QKV:
+            act_ref[columns, :] = projected.astype(BF16)
+            inner[pl.ds(r, 1), pl.ds(x, 1), columns, :] = og[columns, :][None, None]
+        else:
+            normal_cdf = 0.5 * (1.0 + lax.erf(projected * 0.7071067811865476))
+            density = jnp.exp(-0.5 * projected * projected) * 0.3989422804014327
+            act_ref[columns, :] = (projected * normal_cdf).astype(BF16)
+            inner[pl.ds(r, 1), pl.ds(x, 1), columns, :] = (
+                og[columns, :].astype(F32) * (normal_cdf + projected * density)
+            ).astype(BF16)[None, None]
+
+    def inner_x(step, source, i):
+        piece = inner.at[r, source, pl.ds(i * PART, PART), :]
+        return remote(piece, piece, ix_send.at[step, i], ix_recv.at[source, i], dp=at_x(step))
+
+    def activate(step):
+        @pl.when(completed(step) == x)
         def _():
-            proj_own[...] = total
-
-        @pl.when(group != x)
-        def _():
-            proj_tx[index] = total.astype(BF16)
-            proj_copy(group, index).start()
-
-    def proj_copy(group, index):
-        return remote(
-            proj_tx.at[index], proj_rx.at[x], px_send.at[index], px_recv.at[x], dp=group
-        )
+            for i in range(PARTS):
+                for other in range(1, NX):
+                    proj_wait(at_x(other), i)
+                cuts = [i * PART, (i + 1) * PART]
+                if cuts[0] < QKV < cuts[1]:
+                    cuts.insert(1, QKV)
+                for low, high in zip(cuts[:-1], cuts[1:]):
+                    activate_rows(low, high)
+                for other in range(1, NX):
+                    inner_x(other, x, i).start()
 
     sign = 1 - 2 * b
 
@@ -271,28 +318,11 @@
         project(completed(step), step - 1)
         if step < 4:
             turn(step)
-
-    for step in range(1, NX):
-        remote(
-            proj_tx.at[0], proj_rx.at[at_x(step)], px_send.at[0], px_recv.at[at_x(step)], dp=at_x(step)
-        ).wait_recv()
-    projected = proj_own[...]
-    for step in range(1, NX):
-        projected = projected + proj_rx[at_x(step)].astype(F32)
-    og_copy.wait()
-    act_ref[0:QKV, :] = projected[0:QKV].astype(BF16)
-    inner[pl.ds(r, 1), pl.ds(x, 1), 0:QKV, :] = og[0:QKV, :][None, None]
-    hidden = projected[QKV:]
-    normal_cdf = 0.5 * (1.0 + lax.erf(hidden * 0.7071067811865476))
-    density = jnp.exp(-0.5 * hidden * hidden) * 0.3989422804014327
-    act_ref[QKV:, :] = (hidden * normal_cdf).astype(BF16)
-    inner[pl.ds(r, 1), pl.ds(x, 1), QKV:, :] = (
-        og[QKV:, :].astype(F32) * (normal_cdf + hidden * density)
-    ).astype(BF16)[None, None]
-
-    def inner_x(step, source):
-        piece = inner.at[r, source]
-        return remote(piece, piece, ix_send.at[step], inner_recv.at[r, source], dp=at_x(step))
+        if step == 2:
+            og_copy.wait()
+        if step > 2:
+            activate(step - 2)
+    activate(3)
 
     def inner_lo(replica, group):
         piece = inner.at[replica, group]
@@ -307,24 +337,27 @@
             replica=other_core,
         )
 
-    for step in range(1, NX):
-        start(inner_x(step, x))
-    start(inner_lo(r, x))
-    start(inner_core(r, x))
-    for step in (1, 3, 2):
-        inner_x(step, at_x(step)).wait_recv()
-        start(inner_lo(r, at_x(step)))
-        start(inner_core(r, at_x(step)))
-
     def every(replica):
         return jnp.concatenate([inner[replica, g] for g in range(NX)], axis=1)
 
 
-    part[...] = jnp.dot(w_turned[...], every(r), preferred_element_type=F32)
+    def take_group(step):
+        group = completed(step)
+
+        @pl.when(group != x)
+        def _():
+            for i in range(PARTS):
+                inner_x(1, group, i).wait_recv()
+
+        start(inner_lo(r, group))
+        start(inner_core(r, group))
+        part[:, pl.ds(pl.multiple_of(group * TOK, TOK), TOK)] = jnp.dot(
+            w_turned[...], inner[r, group], preferred_element_type=F32
+        )
 
     def part_of(target, k):
         start_row = pl.multiple_of(lax.rem(target, 2) * HALF + at_z(k) * FEAT, FEAT)
-        lane = pl.multiple_of((target // 2) * TOK, TOK)
+        lane = pl.multiple_of(lax.rem(target // 2 + 2, NX) * TOK, TOK)
         return part[pl.ds(start_row, FEAT), pl.ds(lane, TOK)]
 
     def ring_copy(way, h, k):
@@ -359,24 +392,25 @@
     def weight_piece(left, right):
         return lax.dot_general(left, right, (((1,), (1,)), ((), ())), preferred_element_type=F32)
 
-    def add_weight(replica):
+    def wait_rows(replica, features):
         for g in range(NX):
-            remote(
-                normed.at[0], site_rows.at[replica, g], site_send.at[0, 0], site_recv.at[replica, g],
-                replica=other_core,
-            ).wait_recv()
-        left = every(replica)
-        for k in range(PIECES):
-            piece = slice(k * CHUNK, (k + 1) * CHUNK)
-            w_sum[k] += weight_piece(left, rows_of(replica, piece))
+            site_copy(replica, 2 * g, other_core, features).wait_recv()
+
+    def near_piece(k):
+        piece = slice(k * CHUNK, (k + 1) * CHUNK)
+        w_sum[k] = weight_piece(every(r), own_rows(piece))
+        w_sum[k] += weight_piece(every(other_core), rows_of(other_core, piece))
+
+    def sum_copy():
+        return remote(lo_tx, lo_rx, sum_send.at[0], sum_recv.at[0], replica=other_lo)
 
     def wait_inner(replica):
         for g in range(NX):
             inner_core(replica, g).wait_recv()
 
     def pass_on(step):
-        inner_lo(other_lo, at_x(step)).wait_recv()
-        start(inner_core(other_lo, at_x(step)))
+        inner_lo(other_lo, completed(step)).wait_recv()
+        start(inner_core(other_lo, completed(step)))
 
     def done_copy(k, half):
         return remote(
@@ -395,33 +429,23 @@
         out_copies.append(copy)
 
     order = (1, 3, 2, 0)
+    take_group(1)
     ring_round(4, order)
-    for k in order:
-        for way in range(2):
-            if k % 2 != way:
-                ring_send(way, 3, k)
-    for k in range(PIECES):
-        w_sum[k] = weight_piece(every(r), own_rows(slice(k * CHUNK, (k + 1) * CHUNK)))
-    pass_on(0)
-    for k in order:
-        for way in range(2):
-            if k % 2 == way:
-                ring_send(way, 3, k)
-    wait_inner(other_core)
-    add_weight(other_core)
-    ring_round(2, order[:2])
-    pass_on(1)
-    ring_round(2, order[2:])
-    pass_on(3)
-    ring_round(1, order[:2])
-    pass_on(2)
-    ring_round(1, order[2:])
-    add_weight(other_lo)
-
+    activate(4)
+    take_group(2)
+    ring_round(3, order)
+    take_group(3)
+    ring_round(2, order)
+    take_group(4)
+    ring_round(1, order)
     def scatter_z(step, source):
         return remote(
             ztx.at[step], zrx.at[source], zs_send.at[step], zs_recv.at[source], mp=mp(y, at_z(step))
         )
+
+    back_copy = remote(
+        last_tx, ng_ref, perm_send.at[1], perm_recv.at[1], dp=back_x, mp=mp(y_back, z)
+    )
 
     for k in order:
         for way in range(2):
@@ -430,42 +454,62 @@
         if k:
             ztx[k] = total.astype(BF16)
             start(scatter_z(k, z))
-    wait_inner(across)
-    add_weight(across)
+
+    pass_on(1)
+    pass_on(2)
+    wait_inner(other_core)
+    wait_rows(other_core, HALF)
+    near_piece(PIECES - 1)
+    lo_tx[...] = w_sum[PIECES - 1].astype(BF16)
+    start(sum_copy())
     for step in range(1, NZ):
         scatter_z(step, at_z(step)).wait_recv()
         total = total + zrx[at_z(step)].astype(F32)
-
-    @pl.when(moves)
-    def _():
-        last_tx[...] = total.astype(BF16)
-        back_copy().start()
-
-    @pl.when(jnp.logical_not(moves))
-    def _():
-        ng_ref[...] = total.astype(BF16)
-
-    for k in range(PIECES):
-        done[pl.ds(c, 1), k] = (w_sum[k] * 0.25).astype(BF16)[None]
+    last_tx[...] = total.astype(BF16)
+    start(back_copy)
+    for k in range(FAR):
+        near_piece(k)
+    pass_on(3)
+    pass_on(4)
+    wait_rows(other_lo, FAR * CHUNK)
+    for k in range(FAR):
+        w_far[k] = weight_piece(every(other_lo), rows_of(other_lo, slice(k * CHUNK, (k + 1) * CHUNK)))
+    wait_inner(across)
+    wait_rows(across, FAR * CHUNK)
+
+    def finish(k, total):
+        done[pl.ds(c, 1), k] = (total * 0.25).astype(BF16)[None]
         start(done_copy(k, c))
         out_copy(c, k, 0)
+
+    for k in range(FAR):
+        far = w_far[k] + weight_piece(
+            every(across), rows_of(across, slice(k * CHUNK, (k + 1) * CHUNK))
+        )
+        finish(k, w_sum[k] + far)
+    sum_copy().wait_recv()
+    finish(PIECES - 1, lo_tx[...].astype(F32) + lo_rx[...].astype(F32))
     for k in range(PIECES):
         done_copy(k, 1 - c).wait_recv()
         out_copy(1 - c, k, 1)
 
     @pl.when(moves)
     def _():
-        back_copy().wait_recv()
-        back_copy().wait_send()
         perm_copy().wait_send()
+
 
     for index in range(NX):
         @pl.when(completed(index + 1) != x)
         def _(index=index):
-            proj_copy(completed(index + 1), index).wait_send()
+            for i in range(PARTS):
+                proj_copy(completed(index + 1), index, i).wait_send()
 
     for g in range(NX):
-        site_copy(2 * g + 1 - c, other_core).wait_send()
+        site_copy(r, 2 * g + 1 - c, other_core, HALF).wait_send()
+    for step in range(1, NX):
+        for i in range(PARTS):
+            inner_x(step, x, i).wait_send()
+    back_copy.wait_recv()
     for copy in copies:
         copy.wait_send()
     for copy in out_copies:
@@ -521,6 +565,9 @@
         pltpu.VMEM((NZ, FEAT, TOK), BF16),
         pltpu.VMEM((FEAT, TOK), BF16),
         pltpu.VMEM((PIECES, COLS, CHUNK), F32),
+        pltpu.VMEM((FAR, COLS, CHUNK), F32),
+        pltpu.VMEM((COLS, CHUNK), BF16),
+        pltpu.VMEM((COLS, CHUNK), BF16),
         pltpu.VMEM((2, PIECES, COLS, CHUNK), BF16),
         dma((2,)),
         dma((2, PIECES)),
@@ -534,9 +581,10 @@
         dma((2, 4, NZ)),
         dma((2, NY)),
         dma((4, NX)),
-        dma((NX,)),
-        dma((NX,)),
-        dma((NX,)),
+        dma((NX, PARTS)),
+        dma((NX, PARTS)),
+        dma((NX, PARTS)),
+        dma((NX, PARTS)),
         dma((NX,)),
         dma((2, NX)),
         dma((4, NX)),
@@ -544,6 +592,8 @@
         dma((2, 4, NZ)),
         dma((NZ,)),
         dma((NZ,)),
+        dma((1,)),
+        dma((1,)),
         dma((PIECES,)),
         dma((PIECES,)),
     ]

time: 98 us -> 90.2 us (0.920)
  the two profiles are of different devices: /device:TPU:4 before, /device:TPU:1 now
where the time goes in v3:
time: 90.2 us; the launch traced here: 90 us
  Pallas kernels  89.2 us (99%)
    pallas_call x1, Pallas kernels, local(): pl.pallas_call(kernel, out_shape=shapes, in_specs=[vmem, vmem, anywhere,...  86.6 us
    pallas_call x1, Pallas kernels, local(): pl.pallas_call(hand_over, out_shape=shapes, in_specs=[anywhere] * 3, out_...  2.54 us

profile of v3, /device:TPU:1, one launch (start us, length us, event | category | flops | bytes accessed | tf_op | source)
XLA Modules:
  0.0 90.0 jit_solution(12995465268806549666)
XLA Ops:
  0.6 86.6 %shard_map.67 = (bf16[672,128]{1,0:T(8,128)(2,1)}, bf16[192,128]{1,0:T(8,128)(2,1)}, bf16[672,1536]{1,0:T(8,128)(2,1)}) custom-call(bf16[192,128]{1,0:T(8,128)(2,1)} %bitcast.11, bf16[48,128]{1,0:T(8,128)(2,1)} %bitcast.13, bf16[672,128]{1,0:T(8,128)(2,1)} %bitcast.9, bf16[672,1536]{1,0:T(8,128)(2,1)} %bitcast.7), custom_call_target="tpu_custom_call" | custom-call | flops 3200000000 | bytes 5000000 | tf_op jit(solution)/shard_map/pallas_call | solution.py:605
  87.3 2.5 %shard_map.68 = (bf16[672,128]{1,0:T(8,128)(2,1)}, bf16[192,128]{1,0:T(8,128)(2,1)}, bf16[672,1536]{1,0:T(8,128)(2,1)}) custom-call(bf16[672,128]{1,0:T(8,128)(2,1)} %get-tuple-element.9.act_in, bf16[192,128]{1,0:T(8,128)(2,1)} %get-tuple-element.10.ng_in, bf16[672,1536]{1,0:T(8,128)(2,1)} %get-tuple-element.11.wg_in), custom_call_target="tpu_custom_call" | custom-call | bytes 4600000 | tf_op jit(solution)/shard_map/pallas_call | solution.py:621

commit v4 on v3

--- a/solution.py
+++ b/solution.py
@@ -21,8 +21,8 @@
 CHUNK = 256
 PIECES = HALF // CHUNK
 FAR = 2
-PARTS = 3
-PART = COLS // PARTS
+PIECE = 176
+PADDED = NX * PIECE
 
 
 def remote(src, dst, send_sem, recv_sem, **device):
@@ -52,12 +52,12 @@
 
 
 def kernel(
-    tok_ref, gain_ref, og_hbm, w_hbm, act_ref, ng_ref, wg_hbm,
-    w, w_turned, og, gain_rows, gain, stat_z_tx, stat_y_tx, stat_z, stat_y, stat_x, rows, normed,
-    site_rows, proj_tx, proj_rx, proj_own, inner, part, ytx, yrx, ztx, zrx, last_tx,
+    tok_hbm, gain_hbm, og_hbm, w_hbm, act_ref, ng_ref, wg_hbm,
+    tok_ref, gain_ref, w, w_turned, og, og_rx, gain_rows, gain, stat_z_tx, stat_y_tx, stat_z, stat_y, stat_x, rows, normed,
+    site_rows, proj_tx, proj_rx, proj_own, act_tx, act_all, inner, part, ytx, yrx, ztx, zrx, last_tx,
     w_sum, w_far, lo_tx, lo_rx, done,
     w_sem, out_sem, stat_send, stat_recv, perm_send, perm_recv, zg_send, zg_recv,
-    yg_send, yg_recv, site_send, site_recv, px_send, px_recv, ix_send, ix_recv, lo_send, core_send, inner_recv,
+    yg_send, yg_recv, site_send, site_recv, og_send, og_recv, px_send, px_recv, ix_send, ix_recv, act_send, act_recv, lo_send, core_send, inner_recv,
     ys_send, ys_recv, zs_send, zs_recv, sum_send, sum_recv, fin_send, fin_recv,
 ):
     r = lax.axis_index("replica")
@@ -94,6 +94,11 @@
         copies.append(copy)
         copy.start()
 
+    tok_copy = pltpu.make_async_copy(tok_hbm, tok_ref, w_sem.at[2])
+    gain_copy = pltpu.make_async_copy(gain_hbm, gain_ref, w_sem.at[3])
+    tok_copy.start()
+    gain_copy.start()
+
     barrier = pltpu.get_barrier_semaphore()
     greeted = [{"mp": mp(y, at_z(step))} for step in range(1, NZ)]
     greeted += [{"mp": mp(at_y(step), z)} for step in range(1, NY)]
@@ -110,10 +115,11 @@
         )
 
     w_copy = pltpu.make_async_copy(w_hbm, w, w_sem.at[0])
-    og_copy = pltpu.make_async_copy(og_hbm, og, w_sem.at[1])
+    og_copy = pltpu.make_async_copy(og_hbm, og.at[pl.ds(0, COLS), :], w_sem.at[1])
     w_copy.start()
     og_copy.start()
 
+    tok_copy.wait()
     values = tok_ref[...].astype(F32)
     mean = jnp.mean(values, axis=0, keepdims=True)
     squares = jnp.sum(jnp.square(values - mean), axis=0, keepdims=True)
@@ -159,6 +165,30 @@
     def _():
         rows[pl.ds(y, 1), pl.ds(pl.multiple_of(z * FEAT, FEAT), FEAT), :] = tok_ref[...][None]
 
+    def quarter(place):
+        return pl.ds(pl.multiple_of(place * PIECE, 16), PIECE)
+
+    def og_spread(step, source):
+        return remote(
+            og.at[quarter(at_x(step)), :], og_rx.at[source], og_send.at[step], og_recv.at[source],
+            dp=at_x(step),
+        )
+
+    nothing = jnp.zeros((PADDED - COLS, TOK), F32)
+    og[COLS:, :] = nothing.astype(BF16)
+    for index in range(NX):
+        proj_own[index, COLS:, :] = nothing
+        proj_tx[index, COLS:, :] = nothing.astype(BF16)
+    og_copy.wait()
+    og_rx[pl.ds(x, 1)] = og[quarter(x), :][None]
+    for step in range(1, NX):
+        start(og_spread(step, x))
+
+    def turn(piece):
+        columns = slice(piece * HALF // 2, (piece + 1) * HALF // 2)
+        w_turned[columns, :] = jnp.transpose(w[:, columns])
+
+    gain_copy.wait()
     gain_rows[...] = gain_ref[...].astype(F32)
     table = jnp.transpose(
         jnp.concatenate([gain_rows[pl.ds(12 * x, 12), :], jnp.zeros((116, 128), F32)], axis=0)
@@ -173,6 +203,9 @@
     stat_y[pl.ds(y, 1)] = stats[None]
     for step in range(1, NY):
         start(stat_y_copy(step, y))
+    w_copy.wait()
+    turn(0)
+    turn(1)
 
     @pl.when(moves)
     def _():
@@ -194,25 +227,28 @@
         start(gather_z(step, z))
     for way in range(2):
         start(gather_y(way, 0, 0, y))
+    turn(2)
     for step in range(1, NY):
         stat_y_copy(step, at_y(step)).wait_recv()
     stat_x[pl.ds(x, 1)] = merge_stats(stat_y[...], float(HALF))[None]
     for step in range(1, NX):
         start(stat_x_copy(step, x))
-    for k in range(1, NZ):
+    turn(3)
+
+    def receive(step, k):
+        for way in range(2):
+            if step < 4 or k % 2 == way:
+                source = at_y(-step if way == 0 else step)
+                gather_y(way, step - 1, k, source).wait_recv()
+                if step < 3 or (step == 3 and k % 2 == way):
+                    start(gather_y(way, step, k, source))
+
+    arrivals = (0, 1, 3, 2)
+    receive(1, 0)
+    for k in arrivals[1:]:
         gather_z(k, at_z(k)).wait_recv()
         for way in range(2):
             start(gather_y(way, 0, k, y))
-    w_copy.wait()
-
-    def turn(piece):
-        columns = slice(piece * HALF // 2, (piece + 1) * HALF // 2)
-        w_turned[columns, :] = jnp.transpose(w[:, columns])
-
-    turn(0)
-    for step in range(1, NX):
-        stat_x_copy(step, at_x(step)).wait_recv()
-
     def site_copy(source, t, replica, features):
         piece = pl.ds(0, features)
         return remote(
@@ -233,126 +269,123 @@
         def _():
             site_copy(r, t, other_core, HALF).start()
 
-    def project(group, index):
-        for i in range(PARTS):
-            columns = slice(i * PART, (i + 1) * PART)
-            total = jnp.dot(
-                w[columns, :HALF], normed[2 * group], preferred_element_type=F32
-            ) + jnp.dot(w[columns, HALF:], normed[2 * group + 1], preferred_element_type=F32)
-
-            @pl.when(group == x)
-            def _(columns=columns, total=total):
-                proj_own[columns, :] = total
-
-            @pl.when(group != x)
-            def _(i=i, columns=columns, total=total):
-                proj_tx[index, columns, :] = total.astype(BF16)
-                proj_copy(group, index, i).start()
-
-    def proj_copy(group, index, i):
-        columns = pl.ds(i * PART, PART)
-        return remote(
-            proj_tx.at[index, columns, :], proj_rx.at[x, columns, :],
-            px_send.at[index, i], px_recv.at[x, i], dp=group,
-        )
-
-    def proj_wait(source, i):
-        columns = pl.ds(i * PART, PART)
-        remote(
-            proj_tx.at[0, columns, :], proj_rx.at[source, columns, :],
-            px_send.at[0, i], px_recv.at[source, i], dp=source,
-        ).wait_recv()
-
-    def activate_rows(low, high):
-        columns = slice(low, high)
-        projected = proj_own[columns, :]
-        for step in range(1, NX):
-            projected = projected + proj_rx[at_x(step), columns, :].astype(F32)
-        if high <= QKV:
-            act_ref[columns, :] = projected.astype(BF16)
-            inner[pl.ds(r, 1), pl.ds(x, 1), columns, :] = og[columns, :][None, None]
-        else:
-            normal_cdf = 0.5 * (1.0 + lax.erf(projected * 0.7071067811865476))
-            density = jnp.exp(-0.5 * projected * projected) * 0.3989422804014327
-            act_ref[columns, :] = (projected * normal_cdf).astype(BF16)
-            inner[pl.ds(r, 1), pl.ds(x, 1), columns, :] = (
-                og[columns, :].astype(F32) * (normal_cdf + projected * density)
-            ).astype(BF16)[None, None]
-
-    def inner_x(step, source, i):
-        piece = inner.at[r, source, pl.ds(i * PART, PART), :]
-        return remote(piece, piece, ix_send.at[step, i], ix_recv.at[source, i], dp=at_x(step))
+    def project(step, low, high):
+        group = completed(step)
+        total = jnp.dot(
+            w[low:high, :HALF], normed[2 * group], preferred_element_type=F32
+        ) + jnp.dot(w[low:high, HALF:], normed[2 * group + 1], preferred_element_type=F32)
+        proj_own[step - 1, low:high, :] = total
+        proj_tx[step - 1, low:high, :] = total.astype(BF16)
+
+    def proj_copy(step, other, source):
+        return remote(
+            proj_tx.at[step - 1, quarter(at_x(other)), :], proj_rx.at[step - 1, source],
+            px_send.at[step - 1, other], px_recv.at[step - 1, source], dp=at_x(other),
+        )
+
+    def spread(step):
+        for other in range(1, NX):
+            start(proj_copy(step, other, x))
+
+    def inner_x(step, other, source):
+        piece = inner.at[r, completed(step), quarter(source), :]
+        return remote(
+            piece, piece, ix_send.at[step - 1, other], ix_recv.at[step - 1, source], dp=at_x(other)
+        )
+
+    def act_copy(step, source, to):
+        return remote(
+            act_tx.at[step - 1], act_all.at[quarter(source), :],
+            act_send.at[step - 1], act_recv.at[source], dp=to,
+        )
 
     def activate(step):
-        @pl.when(completed(step) == x)
+        group = completed(step)
+        for other in range(1, NX):
+            proj_copy(step, other, at_x(other)).wait_recv()
+        projected = proj_own[step - 1, quarter(x), :]
+        for other in range(1, NX):
+            projected = projected + proj_rx[step - 1, at_x(other)].astype(F32)
+        linear = lax.broadcasted_iota(jnp.int32, (PIECE, TOK), 0) + x * PIECE < QKV
+        normal_cdf = 0.5 * (1.0 + lax.erf(projected * 0.7071067811865476))
+        density = jnp.exp(-0.5 * projected * projected) * 0.3989422804014327
+        slopes = jnp.where(linear, 1.0, normal_cdf + projected * density)
+        inner[pl.ds(r, 1), pl.ds(group, 1), quarter(x), :] = (
+            og_rx[group].astype(F32) * slopes
+        ).astype(BF16)[None, None]
+        for other in range(1, NX):
+            start(inner_x(step, other, x))
+        act_tx[step - 1] = jnp.where(linear, projected, projected * normal_cdf).astype(BF16)
+
+        @pl.when(group != x)
         def _():
-            for i in range(PARTS):
-                for other in range(1, NX):
-                    proj_wait(at_x(other), i)
-                cuts = [i * PART, (i + 1) * PART]
-                if cuts[0] < QKV < cuts[1]:
-                    cuts.insert(1, QKV)
-                for low, high in zip(cuts[:-1], cuts[1:]):
-                    activate_rows(low, high)
-                for other in range(1, NX):
-                    inner_x(other, x, i).start()
+            act_copy(step, x, group).start()
+
+        @pl.when(group == x)
+        def _():
+            act_all[quarter(x), :] = act_tx[step - 1]
 
     sign = 1 - 2 * b
 
     def completed(step):
         return at_y(step * sign if step % 2 else -step * sign) // 2
 
-    normalize(y)
+    def own_row():
+        for step in range(1, NX):
+            stat_x_copy(step, at_x(step)).wait_recv()
+        normalize(y)
+
+    def tasks(step):
+        yield lambda: normalize(at_y(step))
+        if step < 4:
+            yield lambda: normalize(at_y(-step))
+        yield lambda: project(step, 0, COLS // 2)
+        yield lambda: (project(step, COLS // 2, COLS), spread(step))
+        if step == 2:
+            yield wait_og
+        if 1 < step < 4:
+            yield lambda: activate(step - 1)
+
+    def wait_og():
+        for other in range(1, NX):
+            og_spread(other, at_x(other)).wait_recv()
+
+    receive(1, 1)
+    own_row()
+    receive(1, 3)
+    receive(1, 2)
     for step in range(1, 5):
-        for k in range(NZ):
-            for way in range(2):
-                if step == 4 and k % 2 != way:
-                    continue
-                source = at_y(-step if way == 0 else step)
-                gather_y(way, step - 1, k, source).wait_recv()
-                if step < 3 or (step == 3 and k % 2 == way):
-                    start(gather_y(way, step, k, source))
-        normalize(at_y(step))
+        work = list(tasks(step))
         if step < 4:
-            normalize(at_y(-step))
-        project(completed(step), step - 1)
-        if step < 4:
-            turn(step)
-        if step == 2:
-            og_copy.wait()
-        if step > 2:
-            activate(step - 2)
-    activate(3)
+            for k in arrivals:
+                for task in work[:2]:
+                    task()
+                work = work[2:]
+                receive(step + 1, k)
+        for task in work:
+            task()
 
     def inner_lo(replica, group):
-        piece = inner.at[replica, group]
+        piece = inner.at[replica, group, pl.ds(0, COLS), :]
         return remote(
             piece, piece, lo_send.at[group], inner_recv.at[replica, group], replica=other_lo
         )
 
     def inner_core(replica, group):
-        piece = inner.at[replica, group]
+        piece = inner.at[replica, group, pl.ds(0, COLS), :]
         return remote(
             piece, piece, core_send.at[replica // 2, group], inner_recv.at[replica, group],
             replica=other_core,
         )
 
-    def every(replica):
-        return jnp.concatenate([inner[replica, g] for g in range(NX)], axis=1)
-
-
     def take_group(step):
         group = completed(step)
-
-        @pl.when(group != x)
-        def _():
-            for i in range(PARTS):
-                inner_x(1, group, i).wait_recv()
-
+        for other in range(1, NX):
+            inner_x(step, other, at_x(other)).wait_recv()
         start(inner_lo(r, group))
         start(inner_core(r, group))
         part[:, pl.ds(pl.multiple_of(group * TOK, TOK), TOK)] = jnp.dot(
-            w_turned[...], inner[r, group], preferred_element_type=F32
+            w_turned[...], inner[r, group, 0:COLS, :], preferred_element_type=F32
         )
 
     def part_of(target, k):
@@ -383,30 +416,40 @@
                 if h < 4 or k % 2 == way:
                     ring_send(way, h, k)
 
-    def rows_of(replica, piece):
-        return jnp.concatenate([site_rows[replica, g, piece, :] for g in range(NX)], axis=1)
-
-    def own_rows(piece):
-        return jnp.concatenate([normed[2 * g + c, piece, :] for g in range(NX)], axis=1)
-
-    def weight_piece(left, right):
-        return lax.dot_general(left, right, (((1,), (1,)), ((), ())), preferred_element_type=F32)
-
     def wait_rows(replica, features):
         for g in range(NX):
             site_copy(replica, 2 * g, other_core, features).wait_recv()
 
-    def near_piece(k):
+    def weight_piece(left, right):
+        return lax.dot_general(left, right, (((1,), (1,)), ((), ())), preferred_element_type=F32)
+
+    def add_near(step):
+        g = completed(step)
+        inner_core(other_core, g).wait_recv()
+        left = jnp.concatenate([inner[r, g, 0:COLS, :], inner[other_core, g, 0:COLS, :]], axis=1)
+        for k in reversed(range(PIECES)):
+            piece = slice(k * CHUNK, (k + 1) * CHUNK)
+            right = jnp.concatenate(
+                [normed[2 * g + c, piece, :], site_rows[other_core, g, piece, :]], axis=1
+            )
+            w_sum[k] = weight_piece(left, right) + (w_sum[k] if step > 1 else 0.0)
+
+    def far_piece(step, k):
+        g = completed(step)
+        left = jnp.concatenate([inner[other_lo, g, 0:COLS, :], inner[across, g, 0:COLS, :]], axis=1)
         piece = slice(k * CHUNK, (k + 1) * CHUNK)
-        w_sum[k] = weight_piece(every(r), own_rows(piece))
-        w_sum[k] += weight_piece(every(other_core), rows_of(other_core, piece))
+        right = jnp.concatenate(
+            [site_rows[other_lo, g, piece, :], site_rows[across, g, piece, :]], axis=1
+        )
+        return weight_piece(left, right) + (w_far[k] if step > 1 else 0.0)
+
+    def add_far(step):
+        inner_core(across, completed(step)).wait_recv()
+        for k in range(FAR):
+            w_far[k] = far_piece(step, k)
 
     def sum_copy():
         return remote(lo_tx, lo_rx, sum_send.at[0], sum_recv.at[0], replica=other_lo)
-
-    def wait_inner(replica):
-        for g in range(NX):
-            inner_core(replica, g).wait_recv()
 
     def pass_on(step):
         inner_lo(other_lo, completed(step)).wait_recv()
@@ -431,11 +474,15 @@
     order = (1, 3, 2, 0)
     take_group(1)
     ring_round(4, order)
-    activate(4)
+    activate(3)
     take_group(2)
     ring_round(3, order)
+    activate(4)
     take_group(3)
     ring_round(2, order)
+    wait_rows(other_core, HALF)
+    add_near(1)
+    add_near(2)
     take_group(4)
     ring_round(1, order)
     def scatter_z(step, source):
@@ -455,60 +502,55 @@
             ztx[k] = total.astype(BF16)
             start(scatter_z(k, z))
 
+    add_near(3)
+    add_near(4)
+    lo_tx[...] = w_sum[PIECES - 1].astype(BF16)
+    start(sum_copy())
     pass_on(1)
     pass_on(2)
-    wait_inner(other_core)
-    wait_rows(other_core, HALF)
-    near_piece(PIECES - 1)
-    lo_tx[...] = w_sum[PIECES - 1].astype(BF16)
-    start(sum_copy())
+    pass_on(3)
     for step in range(1, NZ):
         scatter_z(step, at_z(step)).wait_recv()
         total = total + zrx[at_z(step)].astype(F32)
     last_tx[...] = total.astype(BF16)
     start(back_copy)
-    for k in range(FAR):
-        near_piece(k)
-    pass_on(3)
+    wait_rows(other_lo, FAR * CHUNK)
+    wait_rows(across, FAR * CHUNK)
+    add_far(1)
+    add_far(2)
     pass_on(4)
-    wait_rows(other_lo, FAR * CHUNK)
-    for k in range(FAR):
-        w_far[k] = weight_piece(every(other_lo), rows_of(other_lo, slice(k * CHUNK, (k + 1) * CHUNK)))
-    wait_inner(across)
-    wait_rows(across, FAR * CHUNK)
+    add_far(3)
 
     def finish(k, total):
         done[pl.ds(c, 1), k] = (total * 0.25).astype(BF16)[None]
         start(done_copy(k, c))
         out_copy(c, k, 0)
 
+    inner_core(across, completed(4)).wait_recv()
     for k in range(FAR):
-        far = w_far[k] + weight_piece(
-            every(across), rows_of(across, slice(k * CHUNK, (k + 1) * CHUNK))
-        )
-        finish(k, w_sum[k] + far)
+        finish(k, w_sum[k] + far_piece(4, k))
     sum_copy().wait_recv()
     finish(PIECES - 1, lo_tx[...].astype(F32) + lo_rx[...].astype(F32))
     for k in range(PIECES):
         done_copy(k, 1 - c).wait_recv()
         out_copy(1 - c, k, 1)
 
+    for other in range(1, NX):
+        act_copy(1, at_x(other), at_x(other)).wait_recv()
+    act_ref[...] = act_all[0:COLS, :]
+
     @pl.when(moves)
     def _():
         perm_copy().wait_send()
 
 
-    for index in range(NX):
-        @pl.when(completed(index + 1) != x)
-        def _(index=index):
-            for i in range(PARTS):
-                proj_copy(completed(index + 1), index, i).wait_send()
+    for step in range(1, 5):
+        @pl.when(completed(step) != x)
+        def _(step=step):
+            act_copy(step, x, completed(step)).wait_send()
 
     for g in range(NX):
         site_copy(r, 2 * g + 1 - c, other_core, HALF).wait_send()
-    for step in range(1, NX):
-        for i in range(PARTS):
-            inner_x(step, x, i).wait_send()
     back_copy.wait_recv()
     for copy in copies:
         copy.wait_send()
@@ -541,9 +583,12 @@
     anywhere = pl.BlockSpec(memory_space=pl.ANY)
     dma = pltpu.SemaphoreType.DMA
     scratch = [
+        pltpu.VMEM((FEAT, TOK), BF16),
+        pltpu.VMEM((D // 128, 128), BF16),
         pltpu.VMEM((COLS, 2 * HALF), BF16),
         pltpu.VMEM((2 * HALF, COLS), BF16),
-        pltpu.VMEM((COLS, TOK), BF16),
+        pltpu.VMEM((PADDED, TOK), BF16),
+        pltpu.VMEM((NX, PIECE, TOK), BF16),
         pltpu.VMEM((D // 128, 128), F32),
         pltpu.VMEM((2 * HALF, TOK), F32),
         pltpu.VMEM((8, 128), F32),
@@ -554,10 +599,12 @@
         pltpu.VMEM((NY, HALF, TOK), BF16),
         pltpu.VMEM((NY, HALF, TOK), BF16),
         pltpu.VMEM((4, NX, HALF, TOK), BF16),
-        pltpu.VMEM((NX, COLS, TOK), BF16),
-        pltpu.VMEM((NX, COLS, TOK), BF16),
-        pltpu.VMEM((COLS, TOK), F32),
-        pltpu.VMEM((4, NX, COLS, TOK), BF16),
+        pltpu.VMEM((NX, PADDED, TOK), BF16),
+        pltpu.VMEM((NX, NX, PIECE, TOK), BF16),
+        pltpu.VMEM((NX, PADDED, TOK), F32),
+        pltpu.VMEM((NX, PIECE, TOK), BF16),
+        pltpu.VMEM((PADDED, TOK), BF16),
+        pltpu.VMEM((4, NX, PADDED, TOK), BF16),
         pltpu.VMEM((2 * HALF, NX * TOK), F32),
         pltpu.VMEM((2, 4, NZ, FEAT, TOK), BF16),
         pltpu.VMEM((2, 4, NZ, FEAT, TOK), BF16),
@@ -569,7 +616,7 @@
         pltpu.VMEM((COLS, CHUNK), BF16),
         pltpu.VMEM((COLS, CHUNK), BF16),
         pltpu.VMEM((2, PIECES, COLS, CHUNK), BF16),
-        dma((2,)),
+        dma((4,)),
         dma((2, PIECES)),
         dma((NZ + NY + NX,)),
         dma((NZ + NY + NX,)),
@@ -581,10 +628,14 @@
         dma((2, 4, NZ)),
         dma((2, NY)),
         dma((4, NX)),
-        dma((NX, PARTS)),
-        dma((NX, PARTS)),
-        dma((NX, PARTS)),
-        dma((NX, PARTS)),
+        dma((NX,)),
+        dma((NX,)),
+        dma((NX, NX)),
+        dma((NX, NX)),
+        dma((NX, NX)),
+        dma((NX, NX)),
+        dma((NX,)),
+        dma((NX,)),
         dma((NX,)),
         dma((2, NX)),
         dma((4, NX)),
@@ -605,7 +656,7 @@
     results = pl.pallas_call(
         kernel,
         out_shape=shapes,
-        in_specs=[vmem, vmem, anywhere, anywhere],
+        in_specs=[anywhere] * 4,
         out_specs=(vmem, vmem, anywhere),
         scratch_shapes=scratch,
         compiler_params=pltpu.CompilerParams(

time: 90.2 us -> 87.8 us (0.973)
  Pallas kernels: 89.2 us -> 87 us
    pallas_call x1, Pallas kernels: 86.6 us -> 84.5 us  [local(): pl.pallas_call(kernel, out_shape=shapes, in_specs=[anywhere] * 4, out_spe...]
where the time goes in v4:
time: 87.8 us; the launch traced here: 87.6 us
  Pallas kernels  87 us (99%)
    pallas_call x1, Pallas kernels, local(): pl.pallas_call(kernel, out_shape=shapes, in_specs=[anywhere] * 4, out_spe...  84.5 us
    pallas_call x1, Pallas kernels, local(): pl.pallas_call(hand_over, out_shape=shapes, in_specs=[anywhere] * 3, out_...  2.54 us

profile of v4, /device:TPU:1, one launch (start us, length us, event | category | flops | bytes accessed | tf_op | source)
XLA Modules:
  0.0 87.6 jit_solution(2570413218352608979)
XLA Ops:
  0.6 84.5 %shard_map.67 = (bf16[672,128]{1,0:T(8,128)(2,1)}, bf16[192,128]{1,0:T(8,128)(2,1)}, bf16[672,1536]{1,0:T(8,128)(2,1)}) custom-call(bf16[192,128]{1,0:T(8,128)(2,1)} %bitcast.11, bf16[48,128]{1,0:T(8,128)(2,1)} %bitcast.13, bf16[672,128]{1,0:T(8,128)(2,1)} %bitcast.9, bf16[672,1536]{1,0:T(8,128)(2,1)} %bitcast.7), custom_call_target="tpu_custom_call" | custom-call | flops 3200000000 | bytes 5000000 | tf_op jit(solution)/shard_map/pallas_call | solution.py:656
  85.1 2.5 %shard_map.68 = (bf16[672,128]{1,0:T(8,128)(2,1)}, bf16[192,128]{1,0:T(8,128)(2,1)}, bf16[672,1536]{1,0:T(8,128)(2,1)}) custom-call(bf16[672,128]{1,0:T(8,128)(2,1)} %get-tuple-element.9.act_in, bf16[192,128]{1,0:T(8,128)(2,1)} %get-tuple-element.10.ng_in, bf16[672,1536]{1,0:T(8,128)(2,1)} %get-tuple-element.11.wg_in), custom_call_target="tpu_custom_call" | custom-call | bytes 4600000 | tf_op jit(solution)/shard_map/pallas_call | solution.py:672

commit v5 on v4

--- a/solution.py
+++ b/solution.py
@@ -53,11 +53,11 @@
 
 def kernel(
     tok_hbm, gain_hbm, og_hbm, w_hbm, act_ref, ng_ref, wg_hbm,
-    tok_ref, gain_ref, w, w_turned, og, og_rx, gain_rows, gain, stat_z_tx, stat_y_tx, stat_z, stat_y, stat_x, rows, normed,
+    tok_ref, gain_ref, w, w_turned, og, og_rx, gain_rows, gain, stat_z_tx, stat_y_tx, stat_z, stat_y, stat_x, site_stat, rows, normed,
     site_rows, proj_tx, proj_rx, proj_own, act_tx, act_all, inner, part, ytx, yrx, ztx, zrx, last_tx,
     w_sum, w_far, lo_tx, lo_rx, done,
     w_sem, out_sem, stat_send, stat_recv, perm_send, perm_recv, zg_send, zg_recv,
-    yg_send, yg_recv, site_send, site_recv, og_send, og_recv, px_send, px_recv, ix_send, ix_recv, act_send, act_recv, lo_send, core_send, inner_recv,
+    yg_send, yg_recv, site_send, site_recv, site_stat_send, site_stat_recv, og_send, og_recv, px_send, px_recv, ix_send, ix_recv, act_send, act_recv, lo_send, core_send, inner_recv,
     ys_send, ys_recv, zs_send, zs_recv, sum_send, sum_recv, fin_send, fin_recv,
 ):
     r = lax.axis_index("replica")
@@ -249,6 +249,19 @@
         gather_z(k, at_z(k)).wait_recv()
         for way in range(2):
             start(gather_y(way, 0, k, y))
+    def raw_copy(t):
+        piece = pl.ds(0, FAR * CHUNK)
+        return remote(
+            rows.at[t, piece, :], site_rows.at[r, t // 2, piece, :],
+            site_send.at[1 - r // 2, t], site_recv.at[r, t // 2],
+            replica=2 * (1 - r // 2) + lax.rem(t, 2),
+        )
+
+    def site_stat_copy(source, to):
+        return remote(
+            stat_x, site_stat.at[source], site_stat_send.at[lax.rem(to, 2)], site_stat_recv.at[source], replica=to
+        )
+
     def site_copy(source, t, replica, features):
         piece = pl.ds(0, features)
         return remote(
@@ -263,7 +276,6 @@
         column = gain[pl.ds(pl.multiple_of(h * HALF, HALF), HALF), :]
         value = (rows[t].astype(F32) - statistics[0:1]) * scale * column
         normed[pl.ds(t, 1)] = value.astype(BF16)[None]
-        start(site_copy(r, t, 2 * (1 - r // 2) + h, FAR * CHUNK))
 
         @pl.when(h != c)
         def _():
@@ -334,6 +346,8 @@
         for step in range(1, NX):
             stat_x_copy(step, at_x(step)).wait_recv()
         normalize(y)
+        for to in (other_lo, across):
+            start(site_stat_copy(r, to))
 
     def tasks(step):
         yield lambda: normalize(at_y(step))
@@ -350,11 +364,15 @@
         for other in range(1, NX):
             og_spread(other, at_x(other)).wait_recv()
 
+    start(raw_copy(y))
     receive(1, 1)
     own_row()
     receive(1, 3)
     receive(1, 2)
     for step in range(1, 5):
+        start(raw_copy(at_y(step)))
+        if step < 4:
+            start(raw_copy(at_y(-step)))
         work = list(tasks(step))
         if step < 4:
             for k in arrivals:
@@ -382,7 +400,8 @@
         group = completed(step)
         for other in range(1, NX):
             inner_x(step, other, at_x(other)).wait_recv()
-        start(inner_lo(r, group))
+        if step < 4:
+            start(inner_lo(r, group))
         start(inner_core(r, group))
         part[:, pl.ds(pl.multiple_of(group * TOK, TOK), TOK)] = jnp.dot(
             w_turned[...], inner[r, group, 0:COLS, :], preferred_element_type=F32
@@ -422,6 +441,18 @@
 
     def weight_piece(left, right):
         return lax.dot_general(left, right, (((1,), (1,)), ((), ())), preferred_element_type=F32)
+
+    def far_rows(replica):
+        site_stat_copy(replica, other_lo).wait_recv()
+        wait_rows(replica, FAR * CHUNK)
+        column = gain[pl.ds(pl.multiple_of(c * HALF, HALF), FAR * CHUNK), :]
+        for g in range(NX):
+            statistics = site_stat[replica, g]
+            scale = lax.rsqrt(statistics[1:2] * (1.0 / D) + 1e-06)
+            value = (
+                site_rows[replica, g, 0 : FAR * CHUNK, :].astype(F32) - statistics[0:1]
+            ) * scale * column
+            site_rows[pl.ds(replica, 1), g, 0 : FAR * CHUNK, :] = value.astype(BF16)[None]
 
     def add_near(step):
         g = completed(step)
@@ -501,12 +532,15 @@
         if k:
             ztx[k] = total.astype(BF16)
             start(scatter_z(k, z))
+    start(inner_lo(r, completed(4)))
 
     add_near(3)
     add_near(4)
     lo_tx[...] = w_sum[PIECES - 1].astype(BF16)
     start(sum_copy())
     pass_on(1)
+    far_rows(other_lo)
+    far_rows(across)
     pass_on(2)
     pass_on(3)
     for step in range(1, NZ):
@@ -514,8 +548,6 @@
         total = total + zrx[at_z(step)].astype(F32)
     last_tx[...] = total.astype(BF16)
     start(back_copy)
-    wait_rows(other_lo, FAR * CHUNK)
-    wait_rows(across, FAR * CHUNK)
     add_far(1)
     add_far(2)
     pass_on(4)
@@ -596,6 +628,7 @@
         pltpu.VMEM((NZ, 8, 128), F32),
         pltpu.VMEM((NY, 8, 128), F32),
         pltpu.VMEM((NX, 8, 128), F32),
+        pltpu.VMEM((4, NX, 8, 128), F32),
         pltpu.VMEM((NY, HALF, TOK), BF16),
         pltpu.VMEM((NY, HALF, TOK), BF16),
         pltpu.VMEM((4, NX, HALF, TOK), BF16),
@@ -628,6 +661,8 @@
         dma((2, 4, NZ)),
         dma((2, NY)),
         dma((4, NX)),
+        dma((2,)),
+        dma((4,)),
         dma((NX,)),
         dma((NX,)),
         dma((NX, NX)),

time: 87.8 us -> 87.3 us (level)
  no operation moved by 1% of the time
where the time goes in v5:
time: 87.3 us; the launch traced here: 87.2 us
  Pallas kernels  86.4 us (99%)
    pallas_call x1, Pallas kernels, local(): pl.pallas_call(kernel, out_shape=shapes, in_specs=[anywhere] * 4, out_spe...  83.8 us
    pallas_call x1, Pallas kernels, local(): pl.pallas_call(hand_over, out_shape=shapes, in_specs=[anywhere] * 3, out_...  2.54 us

profile of v5, /device:TPU:1, one launch (start us, length us, event | category | flops | bytes accessed | tf_op | source)
XLA Modules:
  0.0 87.2 jit_solution(9920806872110396775)
XLA Ops:
  0.6 83.8 %shard_map.67 = (bf16[672,128]{1,0:T(8,128)(2,1)}, bf16[192,128]{1,0:T(8,128)(2,1)}, bf16[672,1536]{1,0:T(8,128)(2,1)}) custom-call(bf16[192,128]{1,0:T(8,128)(2,1)} %bitcast.11, bf16[48,128]{1,0:T(8,128)(2,1)} %bitcast.13, bf16[672,128]{1,0:T(8,128)(2,1)} %bitcast.9, bf16[672,1536]{1,0:T(8,128)(2,1)} %bitcast.7), custom_call_target="tpu_custom_call" | custom-call | flops 3200000000 | bytes 5000000 | tf_op jit(solution)/shard_map/pallas_call | solution.py:691
  84.5 2.5 %shard_map.68 = (bf16[672,128]{1,0:T(8,128)(2,1)}, bf16[192,128]{1,0:T(8,128)(2,1)}, bf16[672,1536]{1,0:T(8,128)(2,1)}) custom-call(bf16[672,128]{1,0:T(8,128)(2,1)} %get-tuple-element.9.act_in, bf16[192,128]{1,0:T(8,128)(2,1)} %get-tuple-element.10.ng_in, bf16[672,1536]{1,0:T(8,128)(2,1)} %get-tuple-element.11.wg_in), custom_call_target="tpu_custom_call" | custom-call | bytes 4600000 | tf_op jit(solution)/shard_map/pallas_call | solution.py:707
